TPU v7x, 128 devices: a whole 4x4x4 slice. The times are simulated.
128 devices in a mesh: blk: 16 (over y, z_lo, core), team: 8 (over z_hi, x).
Axes of the slice: x: 4, y: 4, z: 4 (z_hi: 2, z_lo: 2; z = z_hi * 2 + z_lo), core: 2. Of those that a mesh axis runs over, the one named last changes fastest.
Arguments:
- features: bfloat16 [32768, 128], P(('blk', 'team')), may hold values from -0.796875 to 0.796875
- left_vectors: bfloat16 [32768, 128], P(('blk', 'team')), may hold values from -0.8984375 to 0.8984375
- right_vectors: bfloat16 [32768, 128], P(('blk', 'team')), may hold values from -0.8984375 to 0.8984375
Outputs:
- feature_grad: float32 [32768, 128], P(('blk', 'team'))
All inputs are finite; a program needn't handle non-finite values.
Results may differ from a plain program's by a relative error of at most 0.0039.
Values may be sent and summed in bfloat16 or wider, within the bound.
No kernel may reach another device: no remote copies, remote signals or barrier semaphores. Data moves between devices by JAX's collectives and lax.ppermute only.
A program may use at most 64 MiB of HBM per device.

v0:
```python
import jax
import jax.numpy as jnp
from jax import lax
from jax.sharding import PartitionSpec as P


def pair_block(targets, source_x, source_l, source_r):
    target_x, target_l, target_r, target_norm = targets
    source_norm = jnp.sum(source_x.astype(jnp.float32) ** 2, axis=1)
    cross = jnp.einsum("if,jf->ij", target_x, source_x, preferred_element_type=jnp.float32)
    dist_sq = target_norm[:, None] + source_norm[None, :] - 2.0 * cross
    radius = jnp.sqrt(jnp.maximum(dist_sq, 0.0))
    couple = jnp.einsum(
        "iv,jv->ij", target_l, source_r, preferred_element_type=jnp.float32
    ) + jnp.einsum("iv,jv->ij", target_r, source_l, preferred_element_type=jnp.float32)
    root_five = jnp.float32(5.0) ** 0.5
    weight = (
        -(5.0 / 3.0) * (1.0 + root_five * radius) * jnp.exp(-root_five * radius) * couple
    ).astype(jnp.bfloat16)
    row_total = jnp.sum(weight.astype(jnp.float32), axis=1)
    return row_total[:, None] * target_x.astype(jnp.float32) - jnp.dot(
        weight, source_x, preferred_element_type=jnp.float32
    )


def sweep_sources(running, targets, pieces):
    source_x, source_l, source_r = pieces
    count_rows = source_x.shape[0]
    count_blocks = count_rows // 512

    def one_step(accum, packed):
        return (accum + pair_block(targets, packed[0], packed[1], packed[2]), None)

    stacked = (
        source_x.reshape(count_blocks, 512, -1),
        source_l.reshape(count_blocks, 512, -1),
        source_r.reshape(count_blocks, 512, -1),
    )
    running, unused = lax.scan(one_step, running, stacked)
    return running


def with_norms(target_x, target_l, target_r):
    return (target_x, target_l, target_r, jnp.sum(target_x.astype(jnp.float32) ** 2, axis=1))


def local(features, left_vectors, right_vectors):
    block_x, block_l, block_r = (
        lax.all_gather(features, "team", axis=0, tiled=True),
        lax.all_gather(left_vectors, "team", axis=0, tiled=True),
        lax.all_gather(right_vectors, "team", axis=0, tiled=True),
    )
    targets = with_norms(features, left_vectors, right_vectors)
    start_grad = jnp.zeros(features.shape, jnp.float32)
    return sweep_sources(
        start_grad,
        targets,
        (
            lax.all_gather(block_x, "blk", axis=0, tiled=True),
            lax.all_gather(block_l, "blk", axis=0, tiled=True),
            lax.all_gather(block_r, "blk", axis=0, tiled=True),
        ),
    )


def solution(mesh):
    in_specs = (P(("blk", "team"), None), P(("blk", "team"), None), P(("blk", "team"), None))
    out_specs = P(("blk", "team"), None)
    return jax.shard_map(local, mesh=mesh, in_specs=in_specs, out_specs=out_specs, check_vma=False)
```

profile of v0, /device:TPU:1, one launch (start us, length us, event | category | flops | bytes accessed | tf_op | source)
XLA Modules:
  0.0 600.0 jit_solution(2246003013535040022)
XLA Ops:
  6.5 33.3 %all_gather.18 = bf16[2048,128]{1,0:T(8,128)(2,1)} all-gather(bf16[256,128]{1,0:T(8,128)(2,1)} %param.5), channel_id=1, replica_groups=mesh['blk'=16,'team'=8] {'team'}, dimensions={0}, use_global_device_ids=true | all-gather | bytes 589824 | tf_op jit(solution)/shard_map/all_gather | solution.py:49
  39.9 31.5 %all_gather.20 = bf16[2048,128]{1,0:T(8,128)(2,1)} all-gather(bf16[256,128]{1,0:T(8,128)(2,1)} %param.7), channel_id=1, replica_groups=mesh['blk'=16,'team'=8] {'team'}, dimensions={0}, use_global_device_ids=true | all-gather | bytes 589824 | tf_op jit(solution)/shard_map/all_gather | solution.py:51
  71.5 31.4 %all_gather.22 = bf16[2048,128]{1,0:T(8,128)(2,1)} all-gather(bf16[256,128]{1,0:T(8,128)(2,1)} %param.6), channel_id=1, replica_groups=mesh['blk'=16,'team'=8] {'team'}, dimensions={0}, use_global_device_ids=true | all-gather | bytes 589824 | tf_op jit(solution)/shard_map/all_gather | solution.py:50
  103.9 2.6 all-gather.4.cloned.1.call-done
  106.6 54.0 %all-gather.6.cloned.1.call-done = bf16[32768,128]{1,0:T(8,128)(2,1)} async-done(((bf16[2048,128]{1,0:T(8,128)(2,1)}), bf16[32768,128]{1,0:T(8,128)(2,1)}) %all-gather.6.cloned.1.call-update) | async-done | bytes 8388624 | tf_op jit(solution)/shard_map/all_gather | solution.py:61
  160.6 54.4 %all-gather.8.cloned.1.call-done = bf16[32768,128]{1,0:T(8,128)(2,1)} async-done(((bf16[2048,128]{1,0:T(8,128)(2,1)}), bf16[32768,128]{1,0:T(8,128)(2,1)}) %all-gather.8.cloned.1.call-update) | async-done | bytes 8388624 | tf_op jit(solution)/shard_map/all_gather | solution.py:60
  215.0 377.8 %while.13 = (s32[]{:T(128)}, f32[256,128]{1,0:T(8,128)S(1)}, f32[256]{0:T(256)S(1)}, bf16[64,512,128]{2,1,0:T(8,128)(2,1)}, bf16[256,128]{1,0:T(8,128)(2,1)}, /*...) while((s32[]{:T(128)}, f32[256,128]{1,0:T(8,128)S(1)}, ...), condition=%wide.region_4.5_spmd.clone, body=%wide.region_1.4_spmd.clone.sunk | while | flops 136412416 | bytes 3810427 | solution.py:39
  216.0 1.3 fusion.43
  221.9 1.3 fusion.43
  227.8 1.3 fusion.43
  233.7 1.3 fusion.43
  239.6 1.3 fusion.43
  245.5 1.3 fusion.43
  251.5 1.3 fusion.43
  257.4 1.3 fusion.43
  263.3 1.3 fusion.43
  269.2 1.3 fusion.43
  275.1 1.3 fusion.43
  281.0 1.3 fusion.43
  286.9 1.3 fusion.43
  292.8 1.3 fusion.43
  298.7 1.3 fusion.43
  304.6 1.3 fusion.43
  310.5 1.3 fusion.43
  316.4 1.3 fusion.43
  322.3 1.3 fusion.43
  328.2 1.3 fusion.43
  334.1 1.3 fusion.43
  340.0 1.3 fusion.43
  345.9 1.3 fusion.43
  351.8 1.3 fusion.43
  357.7 1.3 fusion.43
  363.6 1.3 fusion.43
  369.5 1.3 fusion.43
  375.4 1.3 fusion.43
  381.3 1.3 fusion.43
  387.2 1.3 fusion.43
  393.1 1.3 fusion.43
  399.0 1.3 fusion.43
  404.9 1.3 fusion.43
  410.8 1.3 fusion.43
  416.7 1.3 fusion.43
  422.6 1.3 fusion.43
  428.5 1.3 fusion.43
  434.4 1.3 fusion.43
  440.4 1.3 fusion.43
  446.3 1.3 fusion.43
  452.2 1.3 fusion.43
  458.1 1.3 fusion.43
  464.0 1.3 fusion.43
  469.9 1.3 fusion.43
  475.8 1.3 fusion.43
  481.7 1.3 fusion.43
  487.6 1.3 fusion.43
  493.5 1.3 fusion.43
  505.3 1.3 fusion.43
  511.2 1.3 fusion.43
  517.1 1.3 fusion.43
  523.0 1.3 fusion.43
  528.9 1.3 fusion.43
  564.3 1.3 fusion.43
  570.2 1.3 fusion.43
  576.1 1.3 fusion.43
  582.0 1.3 fusion.43
  (273 shorter events, 304.7 us)
Async XLA Ops:
  6.5 100.0 %all-gather.4.cloned.1.call-start = ((), (), s32[]{:S(2)}) async-start(), calls=%async_computation | async-start | bytes 8912896 | tf_op jit(solution)/shard_map/all_gather | solution.py:59
  39.9 120.7 %all-gather.6.cloned.1.call-start = ((), (), s32[]{:S(2)}) async-start(), calls=%async_computation.1 | async-start | bytes 8912896 | tf_op jit(solution)/shard_map/all_gather | solution.py:61
  71.5 143.5 %all-gather.8.cloned.1.call-start = ((), (), s32[]{:S(2)}) async-start(), calls=%async_computation.2 | async-start | bytes 8912896 | tf_op jit(solution)/shard_map/all_gather | solution.py:60
  592.8 0.7 copy-start
Sparse Core Ops, SparseCore 0:
  40.0 66.5 all-gather.3
  108.3 52.2 all-gather.5
  162.3 52.6 all-gather.7
where the time goes:
time: 606 us; the launch traced here: 600 us
  matrix products  307 us (51%)
  waiting for transfers between devices  111 us (18%)
  blocking collectives  96.3 us (16%)
  other arithmetic  68.3 us (11%)
  between operations  13.1 us (2%)
    dot_general x64, matrix products, pair_block(): jnp.einsum('if,jf->ij', target_x, source_x, preferred_element_type=jnp.fl...  80.4 us
    dot_general x64, matrix products, pair_block(): jnp.dot(weight, source_x, preferred_element_type=jnp.float32)  77.7 us
    dot_general x64, matrix products, pair_block(): jnp.einsum('iv,jv->ij', target_r, source_l, preferred_element_type=jnp.fl...  77 us
    dot_general x64, matrix products, pair_block(): jnp.einsum('iv,jv->ij', target_l, source_r, preferred_element_type=jnp.fl...  72.1 us
    reduce_sum x64, other arithmetic, pair_block(): source_norm = jnp.sum(source_x.astype(jnp.float32) ** 2, axis=1)  67.4 us
    all_gather x1, waiting for transfers between devices, local(): lax.all_gather(block_l, 'blk', axis=0, tiled=True)  54.4 us
    all_gather x1, waiting for transfers between devices, local(): lax.all_gather(block_r, 'blk', axis=0, tiled=True)  54 us
    all_gather x1, blocking collectives, local(): lax.all_gather(features, 'team', axis=0, tiled=True)  33.3 us
  transfers between devices with their start and end apart: 3, of which 3 were waited for; matrix products, arithmetic and copies ran while one was open for 0% of the time, Pallas kernels for 0%

commit v1 on v0

v1 whole, which is shorter than its diff:
```python
import functools
import itertools
import math

import jax
import jax.numpy as jnp
import numpy as np
from jax import lax
from jax.experimental import pallas as pl
from jax.experimental.pallas import tpu as pltpu
from jax.sharding import PartitionSpec as P

MEMBERS = (
    ((0, 0, 0), (2, 3, 2), (3, 3, 0), (0, 0, 1), (1, 1, 3), (2, 0, 0), (0, 1, 0), (0, 3, 0)),
    ((0, 0, 0), (1, 0, 3), (0, 0, 2), (0, 3, 1), (1, 2, 0), (3, 1, 0), (0, 2, 0), (3, 0, 0)),
)
BOTH = (
    ((1, 0), (1, 2), (2, 0), (0, 3), (2, 3), (1, 3), (3, 4), (0, 4), (4, 1), (4, 2), (1, 5), (4, 5), (5, 3)),
    ((0, 1), (2, 1), (3, 2), (3, 0), (1, 4), (0, 4), (2, 4), (3, 4), (5, 3), (5, 0), (5, 2), (5, 4), (1, 5)),
)
SINGLE = (
    ((5, 0), (0, 6), (1, 6), (2, 7), (1, 7), (6, 0)),
    ((2, 0), (0, 6), (2, 6), (4, 6), (5, 7), (4, 7)),
)
KEPT = 6
HELD = len(MEMBERS[0])
AXES = ("blk", "team")
ROWS = 512
HALF = 256
FEAT = 128
UNROLL = 4
ROW_TOTAL = FEAT + 3

NEG_RATE = -math.sqrt(5.0) / math.log(2.0)
GAMMA = 1.0 / math.log(2.0)
SCALE = -(5.0 / 3.0) * math.log(2.0)

ROWS_BY_ROWS = (((1,), (1,)), ((), ()))
ROWS_BY_COLUMNS = (((1,), (0,)), ((), ()))


def device_at(x, y, z, core):
    return (((y % 4) * 2 + (z & 1)) * 2 + core) * 8 + ((z % 4) >> 1) * 4 + x % 4


def shift(moves, back=False):
    pairs = []
    for x, y, z, core in itertools.product(range(4), range(4), range(4), range(2)):
        dx, dy, dz = moves[core]
        here, there = device_at(x, y, z, core), device_at(x + dx, y + dy, z + dz, core)
        pairs.append((here, there) if back else (there, here))
    return pairs


def sibling():
    return [
        (device_at(x, y, z, core), device_at(x, y, z, 1 - core))
        for x, y, z, core in itertools.product(range(4), range(4), range(4), range(2))
    ]


def prepare(i, chunk_ref, left_x, right_x, left_v, right_v, turned):
    chunk = chunk_ref[...]
    rows = chunk.shape[0]
    x = chunk[:, :FEAT]
    wide = x.astype(jnp.float32)
    norm = jnp.sum(wide * wide, axis=1, keepdims=True)
    high = norm.astype(jnp.bfloat16).astype(jnp.float32)
    middle = (norm - high).astype(jnp.bfloat16).astype(jnp.float32)
    low = norm - high - middle
    lane = lax.broadcasted_iota(jnp.int32, (rows, FEAT), 1)
    parts = jnp.where(lane % 3 == 0, high, jnp.where(lane % 3 == 1, middle, low))
    left_x[i, :, :FEAT] = (wide * -2.0).astype(jnp.bfloat16)
    left_x[i, :, FEAT:] = jnp.where(lane < 3, 1.0, jnp.where(lane < 6, parts, 0.0)).astype(jnp.bfloat16)
    right_x[i, :, :FEAT] = x
    right_x[i, :, FEAT:] = jnp.where(lane < 3, parts, jnp.where(lane < 6, 1.0, 0.0)).astype(jnp.bfloat16)
    left_v[i] = chunk[:, FEAT:]
    right_v[i, :, :FEAT] = chunk[:, 2 * FEAT :]
    right_v[i, :, FEAT:] = chunk[:, FEAT : 2 * FEAT]
    turned[i, :FEAT, :] = wide.T.astype(jnp.bfloat16)
    row = lax.broadcasted_iota(jnp.int32, (16, rows), 0)
    turned[i, FEAT:, :] = jnp.where(row == ROW_TOTAL - FEAT, 1.0, 0.0).astype(jnp.bfloat16)


def pair_kernel(table, *refs):
    chunks = refs[:HELD]
    own_ref, others_ref = refs[HELD : HELD + 2]
    left_x, right_x, left_v, right_v, turned, total, total_turned = refs[HELD + 2 :]
    for i in range(HELD):
        prepare(i, chunks[i], left_x, right_x, left_v, right_v, turned)
    total[...] = jnp.zeros_like(total)
    total_turned[...] = jnp.zeros_like(total_turned)

    def meet(a, b, first, rows, both):
        strip = pl.ds(first, rows)
        dist_sq = lax.dot_general(
            left_x[a, strip, :], right_x[b], ROWS_BY_ROWS, preferred_element_type=jnp.float32
        )
        couple = lax.dot_general(
            left_v[a, strip, :], right_v[b], ROWS_BY_ROWS, preferred_element_type=jnp.float32
        )
        floor = jnp.maximum(dist_sq, 1e-30)
        u = floor * lax.rsqrt(floor) * NEG_RATE
        weight = ((GAMMA - u) * jnp.exp2(u) * couple).astype(jnp.bfloat16)
        total[a, strip, :] += lax.dot_general(
            weight, right_x[b], ROWS_BY_COLUMNS, preferred_element_type=jnp.float32
        )
        if both:
            total_turned[b] += lax.dot_general(
                turned[a, :, first : first + rows], weight, ROWS_BY_COLUMNS,
                preferred_element_type=jnp.float32,
            )

    def run(first_task, last_task, both):
        def one(s):
            meet(table[2 * s], table[2 * s + 1], 0, ROWS, both)

        looped = (last_task - first_task) // UNROLL * UNROLL

        @pl.loop(first_task, first_task + looped, step=UNROLL)
        def _(s):
            for k in range(UNROLL):
                one(s + k)

        for s in range(first_task + looped, last_task):
            one(s)

    run(0, len(BOTH[0]), True)
    run(len(BOTH[0]), len(BOTH[0]) + len(SINGLE[0]), False)
    meet(0, 0, 0, HALF, False)
    for i in range(KEPT):
        back = total_turned[i].T
        moved = total[i, :, :FEAT] + back[:, :FEAT]
        row_total = total[i, :, ROW_TOTAL : ROW_TOTAL + 1] + back[:, ROW_TOTAL : ROW_TOTAL + 1]
        grad = (row_total * right_x[i, :, :FEAT].astype(jnp.float32) - moved) * SCALE
        if i == 0:
            own_ref[...] = grad
        else:
            others_ref[i - 1] = grad.astype(others_ref.dtype)


def sums_over_pairs(table, chunks):
    whole = pl.BlockSpec(memory_space=pltpu.VMEM)
    stack = pltpu.VMEM((HELD, ROWS, 2 * FEAT), jnp.bfloat16)
    return pl.pallas_call(
        pair_kernel,
        out_shape=(
            jax.ShapeDtypeStruct((ROWS, FEAT), jnp.float32),
            jax.ShapeDtypeStruct((KEPT - 1, ROWS, FEAT), jnp.bfloat16),
        ),
        in_specs=[pl.BlockSpec(memory_space=pltpu.SMEM)] + [whole] * HELD,
        out_specs=(whole, whole),
        scratch_shapes=[stack] * 4
        + [
            pltpu.VMEM((HELD, FEAT + 16, ROWS), jnp.bfloat16),
            pltpu.VMEM((KEPT + 1, ROWS, 2 * FEAT), jnp.float32),
            pltpu.VMEM((KEPT, FEAT + 16, ROWS), jnp.float32),
        ],
        compiler_params=pltpu.CompilerParams(vmem_limit_bytes=48 * 1024 * 1024),
    )(table, *chunks)


def local(features, left_vectors, right_vectors):
    core = lax.axis_index("blk") % 2
    tables = np.array([BOTH[c] + SINGLE[c] for c in range(2)], np.int32).reshape(2, -1)
    table = jnp.where(core == 0, tables[0], tables[1])
    mine = jnp.concatenate([features, left_vectors, right_vectors], axis=1)
    chunk = jnp.concatenate([mine, lax.ppermute(mine, AXES, sibling())], axis=0)
    chunks = [chunk]
    for i in range(1, HELD):
        chunks.append(lax.ppermute(chunk, AXES, shift((MEMBERS[0][i], MEMBERS[1][i]))))
    own, others = sums_over_pairs(table, chunks)
    total = own
    for i in range(1, KEPT):
        back = lax.ppermute(others[i - 1], AXES, shift((MEMBERS[0][i], MEMBERS[1][i]), back=True))
        total = total + back.astype(jnp.float32)
    return total[:HALF] + lax.ppermute(total[HALF:], AXES, sibling())


def solution(mesh):
    spec = P(AXES, None)
    return jax.shard_map(
        local, mesh=mesh, in_specs=(spec, spec, spec), out_specs=spec, check_vma=False
    )
```

time: 606 us -> 82 us (0.14)
  matrix products: 307 us -> 0 us
  blocking collectives: 96.3 us -> 0 us
  waiting for transfers between devices: 111 us -> 24.7 us
  other arithmetic: 68.3 us -> 0.8 us
  starting transfers between devices: 0.09 us -> 36.2 us
  Pallas kernels: 0 us -> 17.6 us
  between operations: 13.1 us -> 0.08 us
    dot_general x256 -> x0, matrix products: 307 us -> none  [the longest x64 80.4 us: pair_block(): jnp.einsum('if,jf->ij', target_x, source_x, preferred_element_type=jnp.fl...]
    all_gather x3 -> x0, waiting for transfers between devices: 111 us -> none  [the longest x1 54.4 us: local(): lax.all_gather(block_l, 'blk', axis=0, tiled=True)]
    all_gather x3 -> x0, blocking collectives: 96.3 us -> none  [the longest x1 33.3 us: local(): lax.all_gather(features, 'team', axis=0, tiled=True)]
    reduce_sum x65 -> x0, other arithmetic: 68.3 us -> none  [the longest x64 67.4 us: pair_block(): source_norm = jnp.sum(source_x.astype(jnp.float32) ** 2, axis=1)]
    ppermute x0 -> x14, starting transfers between devices: none -> 36.2 us  [the longest x5 19 us: local(): lax.ppermute(others[i - 1], AXES, shift((MEMBERS[0][i], MEMBERS[1][i]), b...]
    ppermute x0 -> x14, waiting for transfers between devices: none -> 24.7 us  [the longest x7 15.8 us: local(): lax.ppermute(chunk, AXES, shift((MEMBERS[0][i], MEMBERS[1][i])))]
    pallas_call x0 -> x1, Pallas kernels: none -> 17.6 us  [sums_over_pairs(): pl.pallas_call(pair_kernel, out_shape=(jax.ShapeDtypeStruct((ROWS, FEAT),...]
  transfers between devices with their start and end apart: 3 -> 14, of which waited for: 3 -> 9; matrix products, arithmetic and copies ran while one was open for 0% -> 0% of each run, Pallas kernels for 0% -> 0%
where the time goes in v1:
time: 82 us; the launch traced here: 81.8 us
  starting transfers between devices  36.2 us (44%)
  waiting for transfers between devices  24.7 us (30%)
  Pallas kernels  17.6 us (21%)
  local copies, waits for them, and re-layouts  2.46 us (3%)
    ppermute x5, starting transfers between devices, local(): lax.ppermute(others[i - 1], AXES, shift((MEMBERS[0][i], MEMBERS[1][i]), b...  19 us
    pallas_call x1, Pallas kernels, sums_over_pairs(): pl.pallas_call(pair_kernel, out_shape=(jax.ShapeDtypeStruct((ROWS, FEAT),...  17.6 us
    ppermute x7, waiting for transfers between devices, local(): lax.ppermute(chunk, AXES, shift((MEMBERS[0][i], MEMBERS[1][i])))  15.8 us
    ppermute x7, starting transfers between devices, local(): lax.ppermute(chunk, AXES, shift((MEMBERS[0][i], MEMBERS[1][i])))  12.8 us
    ppermute x5, waiting for transfers between devices, local(): lax.ppermute(others[i - 1], AXES, shift((MEMBERS[0][i], MEMBERS[1][i]), b...  6.8 us
    ppermute x1, starting transfers between devices, local(): return total[:HALF] + lax.ppermute(total[HALF:], AXES, sibling())  2.79 us
    unnamed x10, local copies, waits for them, and re-layouts  2.38 us
  transfers between devices with their start and end apart: 14, of which 9 were waited for; matrix products, arithmetic and copies ran while one was open for 0% of the time, Pallas kernels for 0%

profile of v1, /device:TPU:1, one launch (start us, length us, event | category | flops | bytes accessed | tf_op | source)
XLA Modules:
  0.0 81.8 jit_solution(14605402626970471009)
XLA Ops:
  0.0 0.0 copy-start
  0.0 0.9 %constant_dynamic-update-slice_fusion.2 = bf16[256,384]{1,0:T(8,128)(2,1)S(1)} fusion(bf16[256,128]{1,0:T(8,128)(2,1)} %param.5), kind=kLoop, calls=%fused_computation.10 | loop fusion | bytes 131072
  0.9 0.0 copy-done
  0.9 0.0 copy-start.1
  0.9 0.8 copy-done.1
  1.8 1.5 %collective-permute-start = (bf16[256,384]{1,0:T(8,128)(2,1)S(1)}, bf16[256,384]{1,0:T(8,128)(2,1)S(1)}, u32[]{:S(2)}, u32[]{:S(2)}) collective-permute-start(bf16[256,384]{1,0:T(8,128)(2,1)S(1)} %constant_dynamic-update-slice_fusion), channel_id=1, source_target_pairs={{0,8},{8,0},{16,24},{24,16},{4,12},{12,4},{20,28},{28,20},{32,40},... | collective-permute-start | bytes 589832 | tf_op jit(solution)/shard_map/ppermute | solution.py:168
  3.3 1.1 %collective-permute-done = bf16[256,384]{1,0:T(8,128)(2,1)S(1)} collective-permute-done((bf16[256,384]{1,0:T(8,128)(2,1)S(1)}, bf16[256,384]{1,0:T(8,128)(2,1)S(1)}, u32[]{:S(2)}, u32[]{:S(2)}) %collective-permute-start) | collective-permute-done | bytes 196640 | tf_op jit(solution)/shard_map/ppermute | solution.py:168
  4.4 1.4 %collective-permute-start.7 = (bf16[512,384]{1,0:T(8,128)(2,1)S(1)}, bf16[512,384]{1,0:T(8,128)(2,1)S(1)}, u32[]{:S(2)}, u32[]{:S(2)}) collective-permute-start(bf16[512,384]{1,0:T(8,128)(2,1)S(1)} %pad_maximum_fusion.refs_0_), channel_id=1, source_target_pairs={{96,0},{11,8},{112,16},{27,24},{100,4},{15,12},{116,20},{31,28},{0... | collective-permute-start | bytes 1179656 | tf_op jit(solution)/shard_map/ppermute | solution.py:171
  5.7 2.9 %collective-permute-start.6 = (bf16[512,384]{1,0:T(8,128)(2,1)S(1)}, bf16[512,384]{1,0:T(8,128)(2,1)S(1)}, u32[]{:S(2)}, u32[]{:S(2)}) collective-permute-start(bf16[512,384]{1,0:T(8,128)(2,1)S(1)} %pad_maximum_fusion.refs_0_), channel_id=1, source_target_pairs={{32,0},{72,8},{48,16},{88,24},{36,4},{76,12},{52,20},{92,28},{64,3... | collective-permute-start | bytes 1179656 | tf_op jit(solution)/shard_map/ppermute | solution.py:171
  8.7 1.7 %collective-permute-start.5 = (bf16[512,384]{1,0:T(8,128)(2,1)S(1)}, bf16[512,384]{1,0:T(8,128)(2,1)S(1)}, u32[]{:S(2)}, u32[]{:S(2)}) collective-permute-start(bf16[512,384]{1,0:T(8,128)(2,1)S(1)} %pad_maximum_fusion.refs_0_), channel_id=1, source_target_pairs={{2,0},{43,8},{18,16},{59,24},{6,4},{47,12},{22,20},{63,28},{34,32}... | collective-permute-start | bytes 1179656 | tf_op jit(solution)/shard_map/ppermute | solution.py:171
  10.4 2.6 %collective-permute-start.4 = (bf16[512,384]{1,0:T(8,128)(2,1)S(1)}, bf16[512,384]{1,0:T(8,128)(2,1)S(1)}, u32[]{:S(2)}, u32[]{:S(2)}) collective-permute-start(bf16[512,384]{1,0:T(8,128)(2,1)S(1)} %pad_maximum_fusion.refs_0_), channel_id=1, source_target_pairs={{53,0},{73,8},{33,16},{89,24},{49,4},{77,12},{37,20},{93,28},{85,3... | collective-permute-start | bytes 1179656 | tf_op jit(solution)/shard_map/ppermute | solution.py:171
  13.0 2.2 %collective-permute-start.3 = (bf16[512,384]{1,0:T(8,128)(2,1)S(1)}, bf16[512,384]{1,0:T(8,128)(2,1)S(1)}, u32[]{:S(2)}, u32[]{:S(2)}) collective-permute-start(bf16[512,384]{1,0:T(8,128)(2,1)S(1)} %pad_maximum_fusion.refs_0_), channel_id=1, source_target_pairs={{16,0},{120,8},{4,16},{108,24},{20,4},{124,12},{0,20},{104,28},{48... | collective-permute-start | bytes 1179656 | tf_op jit(solution)/shard_map/ppermute | solution.py:171
  15.2 0.0 collective-permute-done.7.refs_7_
  15.2 1.4 %collective-permute-start.2 = (bf16[512,384]{1,0:T(8,128)(2,1)S(1)}, bf16[512,384]{1,0:T(8,128)(2,1)S(1)}, u32[]{:S(2)}, u32[]{:S(2)}) collective-permute-start(bf16[512,384]{1,0:T(8,128)(2,1)S(1)} %pad_maximum_fusion.refs_0_), channel_id=1, source_target_pairs={{99,0},{12,8},{115,16},{28,24},{103,4},{8,12},{119,20},{24,28},{3,... | collective-permute-start | bytes 1179656 | tf_op jit(solution)/shard_map/ppermute | solution.py:171
  16.6 3.7 %collective-permute-done.6.refs_6_ = bf16[512,384]{1,0:T(8,128)(2,1)S(1)} collective-permute-done((bf16[512,384]{1,0:T(8,128)(2,1)S(1)}, bf16[512,384]{1,0:T(8,128)(2,1)S(1)}, u32[]{:S(2)}, u32[]{:S(2)}) %collective-permute-start.6) | collective-permute-done | bytes 393248 | tf_op jit(solution)/shard_map/ppermute | solution.py:171
  20.2 0.6 collective-permute-start.1
  20.9 0.0 copy-start.2
  20.9 0.0 copy-start.3
  20.9 0.7 copy-done.2
  21.5 0.0 copy-done.3
  21.6 1.3 %collective-permute-done.5.refs_5_ = bf16[512,384]{1,0:T(8,128)(2,1)S(1)} collective-permute-done((bf16[512,384]{1,0:T(8,128)(2,1)S(1)}, bf16[512,384]{1,0:T(8,128)(2,1)S(1)}, u32[]{:S(2)}, u32[]{:S(2)}) %collective-permute-start.5) | collective-permute-done | bytes 393248 | tf_op jit(solution)/shard_map/ppermute | solution.py:171
  22.9 0.7 collective-permute-done.4.refs_4_
  23.6 6.0 %collective-permute-done.3.refs_3_ = bf16[512,384]{1,0:T(8,128)(2,1)S(1)} collective-permute-done((bf16[512,384]{1,0:T(8,128)(2,1)S(1)}, bf16[512,384]{1,0:T(8,128)(2,1)S(1)}, u32[]{:S(2)}, u32[]{:S(2)}) %collective-permute-start.3) | collective-permute-done | bytes 393248 | tf_op jit(solution)/shard_map/ppermute | solution.py:171
  29.6 0.0 collective-permute-done.2.refs_2_
  29.6 4.1 %collective-permute-done.1.refs_1_ = bf16[512,384]{1,0:T(8,128)(2,1)S(1)} collective-permute-done((bf16[512,384]{1,0:T(8,128)(2,1)S(1)}, bf16[512,384]{1,0:T(8,128)(2,1)S(1)}, u32[]{:S(2)}, u32[]{:S(2)}) %collective-permute-start.1) | collective-permute-done | bytes 393248 | tf_op jit(solution)/shard_map/ppermute | solution.py:171
  33.7 17.6 %shard_map.55 = (f32[512,128]{1,0:T(8,128)S(1)}, bf16[5,512,128]{2,1,0:T(8,128)(2,1)S(1)}) custom-call(s32[38]{0:T(128)S(1)} %broadcast_select_fusion.table, bf16[512,384]{1,0:T(8,128)(2,1)S(1)} %pad_maximum_fusion.refs_0_, bf16[512,384]{1,0:T(8,128)(2,1)S(1)} %collective-permute-done.1.refs_1_, bf16[512,384]{1,0:T(8,128)(2,1)S(1)} %collective-permute-done.2.refs_2_, ...), custom_call_target="tpu_custom_call" | custom-call | tf_op jit(solution)/shard_map/pallas_call | solution.py:145
  51.4 0.6 collective-permute-start.8
  52.0 15.9 %collective-permute-start.12 = (bf16[512,128]{1,0:T(8,128)(2,1)S(1)}, bf16[512,128]{1,0:T(8,128)(2,1)S(1)}, u32[]{:S(2)}, u32[]{:S(2)}) collective-permute-start(bf16[512,128]{1,0:T(8,128)(2,1)S(1)} %get-tuple-element.10), channel_id=1, source_target_pairs={{0,2},{8,43},{16,18},{24,59},{4,6},{12,47},{20,22},{28,63},{32,34}... | collective-permute-start | bytes 393224 | tf_op jit(solution)/shard_map/ppermute | solution.py:175
  67.9 2.6 %collective-permute-start.11 = (bf16[512,128]{1,0:T(8,128)(2,1)S(1)}, bf16[512,128]{1,0:T(8,128)(2,1)S(1)}, u32[]{:S(2)}, u32[]{:S(2)}) collective-permute-start(bf16[512,128]{1,0:T(8,128)(2,1)S(1)} %get-tuple-element.11), channel_id=1, source_target_pairs={{0,53},{8,73},{16,33},{24,89},{4,49},{12,77},{20,37},{28,93},{32,8... | collective-permute-start | bytes 393224 | tf_op jit(solution)/shard_map/ppermute | solution.py:175
  70.4 0.0 collective-permute-start.10
  70.4 0.0 collective-permute-start.9
  70.4 0.0 collective-permute-done.8
  70.4 1.9 %collective-permute-done.12 = bf16[512,128]{1,0:T(8,128)(2,1)S(1)} collective-permute-done((bf16[512,128]{1,0:T(8,128)(2,1)S(1)}, bf16[512,128]{1,0:T(8,128)(2,1)S(1)}, u32[]{:S(2)}, u32[]{:S(2)}) %collective-permute-start.12) | collective-permute-done | bytes 131104 | tf_op jit(solution)/shard_map/ppermute | solution.py:175
  72.3 4.9 %collective-permute-done.11 = bf16[512,128]{1,0:T(8,128)(2,1)S(1)} collective-permute-done((bf16[512,128]{1,0:T(8,128)(2,1)S(1)}, bf16[512,128]{1,0:T(8,128)(2,1)S(1)}, u32[]{:S(2)}, u32[]{:S(2)}) %collective-permute-start.11) | collective-permute-done | bytes 131104 | tf_op jit(solution)/shard_map/ppermute | solution.py:175
  77.2 0.0 collective-permute-done.10
  77.2 0.0 collective-permute-done.9
  77.2 0.1 convert_add_fusion
  77.3 2.8 %collective-permute-start.13 = (f32[256,128]{1,0:T(8,128)S(1)}, f32[256,128]{1,0:T(8,128)S(1)}, u32[]{:S(2)}, u32[]{:S(2)}) collective-permute-start(f32[256,128]{1,0:T(8,128)S(1)} %slice.29), channel_id=1, source_target_pairs={{0,8},{8,0},{16,24},{24,16},{4,12},{12,4},{20,28},{28,20},{32,40},... | collective-permute-start | bytes 393224 | tf_op jit(solution)/shard_map/ppermute | solution.py:177
  80.1 1.0 %collective-permute-done.13 = f32[256,128]{1,0:T(8,128)S(1)} collective-permute-done((f32[256,128]{1,0:T(8,128)S(1)}, f32[256,128]{1,0:T(8,128)S(1)}, u32[]{:S(2)}, u32[]{:S(2)}) %collective-permute-start.13) | collective-permute-done | bytes 131104 | tf_op jit(solution)/shard_map/ppermute | solution.py:177
  81.1 0.7 slice_add_fusion
  (6 shorter events, 0.1 us)
Async XLA Ops:
  0.0 0.9 %copy-start = (bf16[256,128]{1,0:T(8,128)(2,1)S(1)}, bf16[256,128]{1,0:T(8,128)(2,1)}, u32[]{:S(2)}) copy-start(bf16[256,128]{1,0:T(8,128)(2,1)} %param.6) | copy-start | bytes 196612
  0.9 0.8 %copy-start.1 = (bf16[256,128]{1,0:T(8,128)(2,1)S(1)}, bf16[256,128]{1,0:T(8,128)(2,1)}, u32[]{:S(2)}) copy-start(bf16[256,128]{1,0:T(8,128)(2,1)} %param.7) | copy-start | bytes 196612
  1.8 2.6 %collective-permute-start = (bf16[256,384]{1,0:T(8,128)(2,1)S(1)}, bf16[256,384]{1,0:T(8,128)(2,1)S(1)}, u32[]{:S(2)}, u32[]{:S(2)}) collective-permute-start(bf16[256,384]{1,0:T(8,128)(2,1)S(1)} %constant_dynamic-update-slice_fusion), channel_id=1, source_target_pairs={{0,8},{8,0},{16,24},{24,16},{4,12},{12,4},{20,28},{28,20},{32,40},... | collective-permute-start | bytes 589832 | tf_op jit(solution)/shard_map/ppermute | solution.py:168
  4.4 10.8 %collective-permute-start.7 = (bf16[512,384]{1,0:T(8,128)(2,1)S(1)}, bf16[512,384]{1,0:T(8,128)(2,1)S(1)}, u32[]{:S(2)}, u32[]{:S(2)}) collective-permute-start(bf16[512,384]{1,0:T(8,128)(2,1)S(1)} %pad_maximum_fusion.refs_0_), channel_id=1, source_target_pairs={{96,0},{11,8},{112,16},{27,24},{100,4},{15,12},{116,20},{31,28},{0... | collective-permute-start | bytes 1179656 | tf_op jit(solution)/shard_map/ppermute | solution.py:171
  5.7 14.5 %collective-permute-start.6 = (bf16[512,384]{1,0:T(8,128)(2,1)S(1)}, bf16[512,384]{1,0:T(8,128)(2,1)S(1)}, u32[]{:S(2)}, u32[]{:S(2)}) collective-permute-start(bf16[512,384]{1,0:T(8,128)(2,1)S(1)} %pad_maximum_fusion.refs_0_), channel_id=1, source_target_pairs={{32,0},{72,8},{48,16},{88,24},{36,4},{76,12},{52,20},{92,28},{64,3... | collective-permute-start | bytes 1179656 | tf_op jit(solution)/shard_map/ppermute | solution.py:171
  8.7 14.2 %collective-permute-start.5 = (bf16[512,384]{1,0:T(8,128)(2,1)S(1)}, bf16[512,384]{1,0:T(8,128)(2,1)S(1)}, u32[]{:S(2)}, u32[]{:S(2)}) collective-permute-start(bf16[512,384]{1,0:T(8,128)(2,1)S(1)} %pad_maximum_fusion.refs_0_), channel_id=1, source_target_pairs={{2,0},{43,8},{18,16},{59,24},{6,4},{47,12},{22,20},{63,28},{34,32}... | collective-permute-start | bytes 1179656 | tf_op jit(solution)/shard_map/ppermute | solution.py:171
  10.4 13.3 %collective-permute-start.4 = (bf16[512,384]{1,0:T(8,128)(2,1)S(1)}, bf16[512,384]{1,0:T(8,128)(2,1)S(1)}, u32[]{:S(2)}, u32[]{:S(2)}) collective-permute-start(bf16[512,384]{1,0:T(8,128)(2,1)S(1)} %pad_maximum_fusion.refs_0_), channel_id=1, source_target_pairs={{53,0},{73,8},{33,16},{89,24},{49,4},{77,12},{37,20},{93,28},{85,3... | collective-permute-start | bytes 1179656 | tf_op jit(solution)/shard_map/ppermute | solution.py:171
  13.0 16.6 %collective-permute-start.3 = (bf16[512,384]{1,0:T(8,128)(2,1)S(1)}, bf16[512,384]{1,0:T(8,128)(2,1)S(1)}, u32[]{:S(2)}, u32[]{:S(2)}) collective-permute-start(bf16[512,384]{1,0:T(8,128)(2,1)S(1)} %pad_maximum_fusion.refs_0_), channel_id=1, source_target_pairs={{16,0},{120,8},{4,16},{108,24},{20,4},{124,12},{0,20},{104,28},{48... | collective-permute-start | bytes 1179656 | tf_op jit(solution)/shard_map/ppermute | solution.py:171
  15.2 14.4 %collective-permute-start.2 = (bf16[512,384]{1,0:T(8,128)(2,1)S(1)}, bf16[512,384]{1,0:T(8,128)(2,1)S(1)}, u32[]{:S(2)}, u32[]{:S(2)}) collective-permute-start(bf16[512,384]{1,0:T(8,128)(2,1)S(1)} %pad_maximum_fusion.refs_0_), channel_id=1, source_target_pairs={{99,0},{12,8},{115,16},{28,24},{103,4},{8,12},{119,20},{24,28},{3,... | collective-permute-start | bytes 1179656 | tf_op jit(solution)/shard_map/ppermute | solution.py:171
  20.2 13.4 %collective-permute-start.1 = (bf16[512,384]{1,0:T(8,128)(2,1)S(1)}, bf16[512,384]{1,0:T(8,128)(2,1)S(1)}, u32[]{:S(2)}, u32[]{:S(2)}) collective-permute-start(bf16[512,384]{1,0:T(8,128)(2,1)S(1)} %pad_maximum_fusion.refs_0_), channel_id=1, source_target_pairs={{102,0},{29,8},{118,16},{9,24},{98,4},{25,12},{114,20},{13,28},{6,... | collective-permute-start | bytes 1179656 | tf_op jit(solution)/shard_map/ppermute | solution.py:171
  20.9 0.7 copy-start.2
  20.9 0.7 copy-start.3
  51.4 19.1 %collective-permute-start.8 = (bf16[512,128]{1,0:T(8,128)(2,1)S(1)}, bf16[512,128]{1,0:T(8,128)(2,1)S(1)}, u32[]{:S(2)}, u32[]{:S(2)}) collective-permute-start(bf16[512,128]{1,0:T(8,128)(2,1)S(1)} %get-tuple-element.9), channel_id=1, source_target_pairs={{0,102},{8,29},{16,118},{24,9},{4,98},{12,25},{20,114},{28,13},{32... | collective-permute-start | bytes 393224 | tf_op jit(solution)/shard_map/ppermute | solution.py:175
  52.0 20.4 %collective-permute-start.12 = (bf16[512,128]{1,0:T(8,128)(2,1)S(1)}, bf16[512,128]{1,0:T(8,128)(2,1)S(1)}, u32[]{:S(2)}, u32[]{:S(2)}) collective-permute-start(bf16[512,128]{1,0:T(8,128)(2,1)S(1)} %get-tuple-element.10), channel_id=1, source_target_pairs={{0,2},{8,43},{16,18},{24,59},{4,6},{12,47},{20,22},{28,63},{32,34}... | collective-permute-start | bytes 393224 | tf_op jit(solution)/shard_map/ppermute | solution.py:175
  67.9 9.4 %collective-permute-start.11 = (bf16[512,128]{1,0:T(8,128)(2,1)S(1)}, bf16[512,128]{1,0:T(8,128)(2,1)S(1)}, u32[]{:S(2)}, u32[]{:S(2)}) collective-permute-start(bf16[512,128]{1,0:T(8,128)(2,1)S(1)} %get-tuple-element.11), channel_id=1, source_target_pairs={{0,53},{8,73},{16,33},{24,89},{4,49},{12,77},{20,37},{28,93},{32,8... | collective-permute-start | bytes 393224 | tf_op jit(solution)/shard_map/ppermute | solution.py:175
  70.4 6.8 %collective-permute-start.10 = (bf16[512,128]{1,0:T(8,128)(2,1)S(1)}, bf16[512,128]{1,0:T(8,128)(2,1)S(1)}, u32[]{:S(2)}, u32[]{:S(2)}) collective-permute-start(bf16[512,128]{1,0:T(8,128)(2,1)S(1)} %get-tuple-element.12), channel_id=1, source_target_pairs={{0,16},{8,120},{16,4},{24,108},{4,20},{12,124},{20,0},{28,104},{32... | collective-permute-start | bytes 393224 | tf_op jit(solution)/shard_map/ppermute | solution.py:175
  70.4 6.8 %collective-permute-start.9 = (bf16[512,128]{1,0:T(8,128)(2,1)S(1)}, bf16[512,128]{1,0:T(8,128)(2,1)S(1)}, u32[]{:S(2)}, u32[]{:S(2)}) collective-permute-start(bf16[512,128]{1,0:T(8,128)(2,1)S(1)} %get-tuple-element.13), channel_id=1, source_target_pairs={{0,99},{8,12},{16,115},{24,28},{4,103},{12,8},{20,119},{28,24},{32... | collective-permute-start | bytes 393224 | tf_op jit(solution)/shard_map/ppermute | solution.py:175
  77.3 3.8 %collective-permute-start.13 = (f32[256,128]{1,0:T(8,128)S(1)}, f32[256,128]{1,0:T(8,128)S(1)}, u32[]{:S(2)}, u32[]{:S(2)}) collective-permute-start(f32[256,128]{1,0:T(8,128)S(1)} %slice.29), channel_id=1, source_target_pairs={{0,8},{8,0},{16,24},{24,16},{4,12},{12,4},{20,28},{28,20},{32,40},... | collective-permute-start | bytes 393224 | tf_op jit(solution)/shard_map/ppermute | solution.py:177

commit v2 on v1

v2 whole, which is shorter than its diff:
```python
import functools
import itertools
import math

import jax
import jax.numpy as jnp
import numpy as np
from jax import lax
from jax.experimental import pallas as pl
from jax.experimental.pallas import tpu as pltpu
from jax.sharding import PartitionSpec as P

MEMBERS = (
    ((0, 0, 0), (0, 3, 1), (0, 3, 3), (3, 0, 1), (1, 1, 0), (2, 0, 1), (0, 2, 3), (0, 0, 3)),
    ((0, 0, 0), (3, 3, 1), (3, 0, 1), (0, 2, 0), (0, 0, 3), (1, 2, 0), (0, 0, 2), (2, 0, 0)),
)
SOURCE = (0, 2, 0, 0, 0, 3, 2, 2)
KEPT = (0, 1, 2, 3, 4, 5)
STAGES = (
    (
        (((0, 4), (2, 0)), ((2, 3), (3, 2), (3, 4), (4, 3))),
        (((2, 0), (4, 3)), ((0, 3), (0, 4), (4, 0), (4, 2))),
    ),
    (
        (((0, 5), (1, 0), (1, 4), (1, 5), (2, 5), (3, 1), (5, 3)), ((2, 1), (4, 5), (5, 4))),
        (((0, 5), (1, 0), (1, 2), (1, 3), (1, 4), (4, 5), (5, 1)), ((2, 5), (5, 2))),
    ),
    (
        ((), ((1, 6), (1, 7), (3, 6), (3, 7), (4, 7), (5, 6), (5, 7))),
        ((), ((0, 7), (1, 6), (2, 6), (2, 7), (3, 6), (3, 7), (5, 6))),
    ),
)
ORDER = (2, 3, 4, 1, 5, 6, 7)
AXES = ("blk", "team")
HELD = len(MEMBERS[0])
ROWS = 512
HALF = 256
FEAT = 128
UNROLL = 4
ROW_TOTAL = FEAT + 3

NEG_RATE = -math.sqrt(5.0) / math.log(2.0)
GAMMA = 1.0 / math.log(2.0)
SCALE = -(5.0 / 3.0) * math.log(2.0)

ROWS_BY_ROWS = (((1,), (1,)), ((), ()))
ROWS_BY_COLUMNS = (((1,), (0,)), ((), ()))


def device_at(x, y, z, core):
    return (((y % 4) * 2 + (z & 1)) * 2 + core) * 8 + ((z % 4) >> 1) * 4 + x % 4


def shift(moves, back=False):
    pairs = []
    for x, y, z, core in itertools.product(range(4), range(4), range(4), range(2)):
        dx, dy, dz = moves[core]
        here, there = device_at(x, y, z, core), device_at(x + dx, y + dy, z + dz, core)
        pairs.append((here, there) if back else (there, here))
    return pairs


def sibling():
    return [
        (device_at(x, y, z, core), device_at(x, y, z, 1 - core))
        for x, y, z, core in itertools.product(range(4), range(4), range(4), range(2))
    ]


class Stage:
    def __init__(self, pairs, with_own):
        both = [pairs[c][0] for c in range(2)]
        single = [pairs[c][1] for c in range(2)]
        every = [p for c in range(2) for p in both[c] + single[c]]
        own = [(0, 0)] if with_own else []
        sums = {a for a, _ in every + own} | {b for c in range(2) for _, b in both[c]}
        used = sums | {b for _, b in every + own}
        self.sums = sorted(sums)
        self.ids = self.sums + sorted(used - sums)
        place = {i: n for n, i in enumerate(self.ids)}
        self.lefts = sorted({place[a] for a, _ in every + own})
        self.rights = sorted({place[b] for _, b in every + own})
        self.turns = sorted({place[a] for c in range(2) for a, _ in both[c]})
        spare = len(self.sums)
        self.slots = max(len(self.ids), spare + 1)
        self.count = [max(len(q[0]), len(q[1])) for q in (both, single)]
        self.with_own = with_own

        def padded(pairs, count):
            local = [(place[a], place[b]) for a, b in pairs]
            return local + [(spare, spare)] * (count - len(local))

        self.table = np.array(
            [padded(both[c], self.count[0]) + padded(single[c], self.count[1]) for c in range(2)],
            np.int32,
        ).reshape(2, -1)


def prepare(i, chunk_ref, stage, left_x, right_x, left_v, right_v, turned):
    chunk = chunk_ref[...]
    rows = chunk.shape[0]
    x = chunk[:, :FEAT]
    wide = x.astype(jnp.float32)
    norm = jnp.sum(wide * wide, axis=1, keepdims=True)
    high = norm.astype(jnp.bfloat16).astype(jnp.float32)
    middle = (norm - high).astype(jnp.bfloat16).astype(jnp.float32)
    low = norm - high - middle
    lane = lax.broadcasted_iota(jnp.int32, (rows, FEAT), 1)
    if i in stage.lefts:
        tail = jnp.where(lane == 3, high, jnp.where(lane == 4, middle, jnp.where(lane == 5, low, 0.0)))
        left_x[i, :, :FEAT] = (wide * -2.0).astype(jnp.bfloat16)
        left_x[i, :, FEAT:] = jnp.where(lane < 3, 1.0, tail).astype(jnp.bfloat16)
        left_v[i] = chunk[:, FEAT:]
    if i in stage.rights:
        tail = jnp.where(lane == 0, high, jnp.where(lane == 1, middle, jnp.where(lane == 2, low, 1.0)))
        right_x[i, :, :FEAT] = x
        right_x[i, :, FEAT:] = jnp.where(lane < 6, tail, 0.0).astype(jnp.bfloat16)
        right_v[i, :, :FEAT] = chunk[:, 2 * FEAT :]
        right_v[i, :, FEAT:] = chunk[:, FEAT : 2 * FEAT]
    if i in stage.turns:
        turned[i, :FEAT, :] = wide.T.astype(jnp.bfloat16)
        row = lax.broadcasted_iota(jnp.int32, (16, rows), 0)
        turned[i, FEAT:, :] = jnp.where(row == ROW_TOTAL - FEAT, 1.0, 0.0).astype(jnp.bfloat16)


def pair_kernel(stage, earlier, table, *refs):
    chunks, refs = refs[: len(stage.ids)], refs[len(stage.ids) :]
    before, refs = dict(zip(earlier, refs)), refs[len(earlier) :]
    out_refs, refs = refs[: len(stage.sums)], refs[len(stage.sums) :]
    left_x, right_x, left_v, right_v, turned, total, total_turned = refs
    for i in range(len(stage.ids)):
        prepare(i, chunks[i], stage, left_x, right_x, left_v, right_v, turned)
    total[...] = jnp.zeros_like(total)
    total_turned[...] = jnp.zeros_like(total_turned)

    def meet(a, b, rows, both):
        dist_sq = lax.dot_general(
            left_x[a, :rows, :], right_x[b], ROWS_BY_ROWS, preferred_element_type=jnp.float32
        )
        couple = lax.dot_general(
            left_v[a, :rows, :], right_v[b], ROWS_BY_ROWS, preferred_element_type=jnp.float32
        )
        floor = jnp.maximum(dist_sq, 1e-30)
        u = floor * lax.rsqrt(floor) * NEG_RATE
        weight = ((GAMMA - u) * jnp.exp2(u) * couple).astype(jnp.bfloat16)
        total[a, :rows, :] += lax.dot_general(
            weight, right_x[b], ROWS_BY_COLUMNS, preferred_element_type=jnp.float32
        )
        if both:
            total_turned[b] += lax.dot_general(
                turned[a], weight, ROWS_BY_COLUMNS, preferred_element_type=jnp.float32
            )

    def run(first_task, last_task, both):
        def one(s):
            meet(table[2 * s], table[2 * s + 1], ROWS, both)

        looped = (last_task - first_task) // UNROLL * UNROLL
        if looped > UNROLL:

            @pl.loop(first_task, first_task + looped, step=UNROLL)
            def _(s):
                for k in range(UNROLL):
                    one(s + k)

        else:
            looped = 0
        for s in range(first_task + looped, last_task):
            one(s)

    if stage.with_own:
        meet(0, 0, HALF, False)
    run(0, stage.count[0], True)
    run(stage.count[0], sum(stage.count), False)
    for i, out_ref in enumerate(out_refs):
        moved = total[i, :, :FEAT]
        row_total = total[i, :, ROW_TOTAL : ROW_TOTAL + 1]
        if stage.count[0]:
            back = total_turned[i].T
            moved = moved + back[:, :FEAT]
            row_total = row_total + back[:, ROW_TOTAL : ROW_TOTAL + 1]
        grad = (row_total * chunks[i][:, :FEAT].astype(jnp.float32) - moved) * SCALE
        if i in before:
            grad = grad + before[i][...]
        out_ref[...] = grad.astype(out_ref.dtype)


def sums_over_pairs(stage, table, chunks, before, kinds):
    whole = pl.BlockSpec(memory_space=pltpu.VMEM)
    stack = pltpu.VMEM((stage.slots, ROWS, 2 * FEAT), jnp.bfloat16)
    sums = len(stage.sums) + 1
    turned_sums = sums if stage.count[0] else 1
    pairs = (stage.count[0] + stage.count[1]) * ROWS * ROWS
    return pl.pallas_call(
        functools.partial(pair_kernel, stage, tuple(before)),
        out_shape=[jax.ShapeDtypeStruct((ROWS, FEAT), kind) for kind in kinds],
        in_specs=[pl.BlockSpec(memory_space=pltpu.SMEM)] + [whole] * (len(chunks) + len(before)),
        out_specs=[whole] * len(kinds),
        scratch_shapes=[stack] * 4
        + [
            pltpu.VMEM((stage.slots, FEAT + 16, ROWS), jnp.bfloat16),
            pltpu.VMEM((sums, ROWS, 2 * FEAT), jnp.float32),
            pltpu.VMEM((turned_sums, FEAT + 16, ROWS), jnp.float32),
        ],
        compiler_params=pltpu.CompilerParams(vmem_limit_bytes=40 * 1024 * 1024),
        cost_estimate=pl.CostEstimate(
            flops=pairs * 2048, bytes_accessed=len(chunks) * ROWS * FEAT * 6, transcendentals=2 * pairs
        ),
    )(table, *chunks, *before.values())


def local(features, left_vectors, right_vectors):
    core = lax.axis_index("blk") % 2
    mine = jnp.concatenate([features, left_vectors, right_vectors], axis=1)
    chunks = [jnp.concatenate([mine, lax.ppermute(mine, AXES, sibling())], axis=0)]
    chunks += [None] * (HELD - 1)
    for i in ORDER:
        moves = [
            tuple(m - n for m, n in zip(MEMBERS[c][i], MEMBERS[c][SOURCE[i]])) for c in range(2)
        ]
        chunks[i] = lax.ppermute(chunks[SOURCE[i]], AXES, shift(moves))
    stages = [Stage(pairs, n == 0) for n, pairs in enumerate(STAGES)]
    sums, own = {}, []
    for n, stage in enumerate(stages):
        table = jnp.where(core == 0, stage.table[0], stage.table[1])
        last = [not any(i in later.sums for later in stages[n + 1 :]) for i in stage.sums]
        kinds = [jnp.bfloat16 if i and done else jnp.float32 for i, done in zip(stage.sums, last)]
        before = {k: sums[i] for k, i in enumerate(stage.sums) if i and i in sums}
        out = sums_over_pairs(stage, table, [chunks[i] for i in stage.ids], before, kinds)
        for i, value in zip(stage.sums, out):
            if i:
                sums[i] = value
            else:
                own.append(value)
    total = functools.reduce(jnp.add, own)
    for i in sums:
        moves = (MEMBERS[0][i], MEMBERS[1][i])
        total = total + lax.ppermute(sums[i], AXES, shift(moves, back=True)).astype(jnp.float32)
    return total[:HALF] + lax.ppermute(total[HALF:], AXES, sibling())


def solution(mesh):
    spec = P(AXES, None)
    return jax.shard_map(
        local, mesh=mesh, in_specs=(spec, spec, spec), out_specs=spec, check_vma=False
    )
```

time: 82 us -> 71.8 us (0.88)
  waiting for transfers between devices: 24.7 us -> 12.9 us
  Pallas kernels: 17.6 us -> 22.8 us
  starting transfers between devices: 36.2 us -> 32.7 us
    ppermute x13, waiting for transfers between devices: 23.7 us -> 11.9 us  [the longest x5 7.64 us: local(): lax.ppermute(sums[i], AXES, shift(moves, back=True)).astype(jnp.float32)]
    ppermute x13, starting transfers between devices: 33.4 us -> 26.6 us  [the longest x7 18.5 us: local(): chunks[i] = lax.ppermute(chunks[SOURCE[i]], AXES, shift(moves))]
    pallas_call x1 -> x3, Pallas kernels: 17.6 us -> 22.8 us  [sums_over_pairs(): pl.pallas_call(functools.partial(pair_kernel, stage, tuple(before)), out_...]
    ppermute x1, starting transfers between devices: 2.79 us -> 6.11 us  [local(): return total[:HALF] + lax.ppermute(total[HALF:], AXES, sibling())]
    unnamed x10 -> x18, local copies, waits for them, and re-layouts: 2.38 us -> 1.75 us
  transfers between devices with their start and end apart: 14 -> 14, of which waited for: 9 -> 6; matrix products, arithmetic and copies ran while one was open for 0% -> 0% of each run, Pallas kernels for 0% -> 23%
where the time goes in v2:
time: 71.8 us; the launch traced here: 71.2 us
  starting transfers between devices  32.7 us (46%)
  Pallas kernels  22.8 us (32%)
  waiting for transfers between devices  12.9 us (18%)
  local copies, waits for them, and re-layouts  1.78 us (2%)
  other arithmetic  0.83 us (1%)
    pallas_call x3, Pallas kernels, sums_over_pairs(): pl.pallas_call(functools.partial(pair_kernel, stage, tuple(before)), out_...  22.8 us
    ppermute x7, starting transfers between devices, local(): chunks[i] = lax.ppermute(chunks[SOURCE[i]], AXES, shift(moves))  18.5 us
    ppermute x5, waiting for transfers between devices, local(): lax.ppermute(sums[i], AXES, shift(moves, back=True)).astype(jnp.float32)  7.64 us
    ppermute x5, starting transfers between devices, local(): lax.ppermute(sums[i], AXES, shift(moves, back=True)).astype(jnp.float32)  6.61 us
    ppermute x1, starting transfers between devices, local(): return total[:HALF] + lax.ppermute(total[HALF:], AXES, sibling())  6.11 us
    ppermute x7, waiting for transfers between devices, local(): chunks[i] = lax.ppermute(chunks[SOURCE[i]], AXES, shift(moves))  3.22 us
    unnamed x18, local copies, waits for them, and re-layouts  1.75 us
    ppermute x1, starting transfers between devices, local(): lax.ppermute(mine, AXES, sibling())  1.5 us
  transfers between devices with their start and end apart: 14, of which 6 were waited for; matrix products, arithmetic and copies ran while one was open for 0% of the time, Pallas kernels for 23%

profile of v2, /device:TPU:1, one launch (start us, length us, event | category | flops | bytes accessed | tf_op | source)
XLA Modules:
  0.0 71.2 jit_solution(2639113950626343629)
XLA Ops:
  0.0 0.0 copy-start
  0.0 0.9 %constant_dynamic-update-slice_fusion.2 = bf16[256,384]{1,0:T(8,128)(2,1)S(1)} fusion(bf16[256,128]{1,0:T(8,128)(2,1)} %param.9), kind=kLoop, calls=%fused_computation.5 | loop fusion | bytes 131072
  0.9 0.0 copy-done
  0.9 0.0 copy-start.1
  0.9 0.8 %copy-done.1 = bf16[256,128]{1,0:T(8,128)(2,1)S(1)} copy-done((bf16[256,128]{1,0:T(8,128)(2,1)S(1)}, bf16[256,128]{1,0:T(8,128)(2,1)}, u32[]{:S(2)}) %copy-start.1) | copy-done | bytes 65560
  1.8 1.5 %collective-permute-start = (bf16[256,384]{1,0:T(8,128)(2,1)S(1)}, bf16[256,384]{1,0:T(8,128)(2,1)S(1)}, u32[]{:S(2)}, u32[]{:S(2)}) collective-permute-start(bf16[256,384]{1,0:T(8,128)(2,1)S(1)} %constant_dynamic-update-slice_fusion), channel_id=1, source_target_pairs={{0,8},{8,0},{16,24},{24,16},{4,12},{12,4},{20,28},{28,20},{32,40},... | collective-permute-start | bytes 589832 | tf_op jit(solution)/shard_map/ppermute | solution.py:215
  3.3 0.0 copy-start.6
  3.3 0.0 copy-start.7
  3.3 1.1 %collective-permute-done = bf16[256,384]{1,0:T(8,128)(2,1)S(1)} collective-permute-done((bf16[256,384]{1,0:T(8,128)(2,1)S(1)}, bf16[256,384]{1,0:T(8,128)(2,1)S(1)}, u32[]{:S(2)}, u32[]{:S(2)}) %collective-permute-start) | collective-permute-done | bytes 196640 | tf_op jit(solution)/shard_map/ppermute | solution.py:215
  4.4 0.0 copy-start.4
  4.4 0.0 copy-start.5
  4.4 3.1 %collective-permute-start.2 = (bf16[512,384]{1,0:T(8,128)(2,1)S(1)}, bf16[512,384]{1,0:T(8,128)(2,1)S(1)}, u32[]{:S(2)}, u32[]{:S(2)}) collective-permute-start(bf16[512,384]{1,0:T(8,128)(2,1)S(1)} %pad_maximum_fusion.refs_0_), channel_id=1, source_target_pairs={{19,0},{72,8},{7,16},{88,24},{23,4},{76,12},{3,20},{92,28},{51,32}... | collective-permute-start | bytes 1179656 | tf_op jit(solution)/shard_map/ppermute | solution.py:221
  7.5 4.7 %collective-permute-start.1 = (bf16[512,384]{1,0:T(8,128)(2,1)S(1)}, bf16[512,384]{1,0:T(8,128)(2,1)S(1)}, u32[]{:S(2)}, u32[]{:S(2)}) collective-permute-start(bf16[512,384]{1,0:T(8,128)(2,1)S(1)} %pad_maximum_fusion.refs_0_), channel_id=1, source_target_pairs={{116,0},{27,8},{96,16},{15,24},{112,4},{31,12},{100,20},{11,28},{2... | collective-permute-start | bytes 1179656 | tf_op jit(solution)/shard_map/ppermute | solution.py:221
  12.2 0.0 copy-done.6
  12.2 0.0 copy-done.7
  12.2 0.0 copy-start.2
  12.2 0.0 copy-start.3
  12.2 0.1 collective-permute-start.3
  12.3 0.0 copy-done.4
  12.3 0.0 copy-done.5
  12.3 1.4 %collective-permute-done.2.refs_2_.refs_3_ = bf16[512,384]{1,0:T(8,128)(2,1)S(1)} collective-permute-done((bf16[512,384]{1,0:T(8,128)(2,1)S(1)}, bf16[512,384]{1,0:T(8,128)(2,1)S(1)}, u32[]{:S(2)}, u32[]{:S(2)}) %collective-permute-start.2) | collective-permute-done | bytes 393248 | tf_op jit(solution)/shard_map/ppermute | solution.py:221
  13.7 3.5 %collective-permute-start.5 = (bf16[512,384]{1,0:T(8,128)(2,1)S(1)}, bf16[512,384]{1,0:T(8,128)(2,1)S(1)}, u32[]{:S(2)}, u32[]{:S(2)}) collective-permute-start(bf16[512,384]{1,0:T(8,128)(2,1)S(1)} %collective-permute-done.2.refs_2_.refs_3_), channel_id=1, source_target_pairs={{3,0},{9,8},{19,16},{25,24},{7,4},{13,12},{23,20},{29,28},{35,32},... | collective-permute-start | bytes 1179656 | tf_op jit(solution)/shard_map/ppermute | solution.py:221
  17.2 1.8 %collective-permute-done.1.refs_1_.refs_2_ = bf16[512,384]{1,0:T(8,128)(2,1)S(1)} collective-permute-done((bf16[512,384]{1,0:T(8,128)(2,1)S(1)}, bf16[512,384]{1,0:T(8,128)(2,1)S(1)}, u32[]{:S(2)}, u32[]{:S(2)}) %collective-permute-start.1) | collective-permute-done | bytes 393248 | tf_op jit(solution)/shard_map/ppermute | solution.py:221
  19.0 1.3 %collective-permute-start.4 = (bf16[512,384]{1,0:T(8,128)(2,1)S(1)}, bf16[512,384]{1,0:T(8,128)(2,1)S(1)}, u32[]{:S(2)}, u32[]{:S(2)}) collective-permute-start(bf16[512,384]{1,0:T(8,128)(2,1)S(1)} %collective-permute-done.1.refs_1_.refs_2_), channel_id=1, source_target_pairs={{4,0},{104,8},{20,16},{120,24},{0,4},{108,12},{16,20},{124,28},{36... | collective-permute-start | bytes 1179656 | tf_op jit(solution)/shard_map/ppermute | solution.py:221
  20.3 0.0 copy-done.2
  20.3 0.0 copy-done.3
  20.3 0.9 %collective-permute-start.7 = (bf16[512,384]{1,0:T(8,128)(2,1)S(1)}, bf16[512,384]{1,0:T(8,128)(2,1)S(1)}, u32[]{:S(2)}, u32[]{:S(2)}) collective-permute-start(bf16[512,384]{1,0:T(8,128)(2,1)S(1)} %collective-permute-done.1.refs_1_.refs_2_), channel_id=1, source_target_pairs={{32,0},{31,8},{48,16},{11,24},{36,4},{27,12},{52,20},{15,28},{64,3... | collective-permute-start | bytes 1179656 | tf_op jit(solution)/shard_map/ppermute | solution.py:221
  21.2 5.0 %collective-permute-start.6 = (bf16[512,384]{1,0:T(8,128)(2,1)S(1)}, bf16[512,384]{1,0:T(8,128)(2,1)S(1)}, u32[]{:S(2)}, u32[]{:S(2)}) collective-permute-start(bf16[512,384]{1,0:T(8,128)(2,1)S(1)} %collective-permute-done.1.refs_1_.refs_2_), channel_id=1, source_target_pairs={{96,0},{25,8},{112,16},{13,24},{100,4},{29,12},{116,20},{9,28},{0,... | collective-permute-start | bytes 1179656 | tf_op jit(solution)/shard_map/ppermute | solution.py:221
  26.2 0.0 collective-permute-done.3.refs_3_.refs_4_
  26.2 6.2 %shard_map.91 = (f32[512,128]{1,0:T(8,128)S(1)}, f32[512,128]{1,0:T(8,128)S(1)}, f32[512,128]{1,0:T(8,128)S(1)}, f32[512,128]{1,0:T(8,128)S(1)}) custom-call(s32[12]{0:T(128)S(1)} %broadcast_select_fusion.2.table, bf16[512,384]{1,0:T(8,128)(2,1)S(1)} %pad_maximum_fusion.refs_0_, bf16[512,384]{1,0:T(8,128)(2,1)S(1)} %collective-permute-done.1.refs_1_.refs_2_, ...), custom_call_target="tpu_custom_call" | custom-call | flops 3221225472 | bytes 1572864 | tf_op jit(solution)/shard_map/pallas_call | solution.py:194
  32.4 0.0 collective-permute-done.5.refs_5_
  32.4 0.0 collective-permute-done.4.refs_1_
  32.5 10.3 %shard_map.92 = (f32[512,128]{1,0:T(8,128)S(1)}, f32[512,128]{1,0:T(8,128)S(1)}, f32[512,128]{1,0:T(8,128)S(1)}, f32[512,128]{1,0:T(8,128)S(1)}, f32[512,128]{1,0:T(8,128)S(1)}, /*index=5*/f32[512,128]{1,0:T(8,128)S(1)}) custom-call(s32[20]{0:T(128)S(1)} %broadcast_select_fusion.1.table, bf16[512,384]{1,0:T(8,128)(2,1)S(1)} %pad_maximum_fusion.refs_0_, ...), custom_call_target="tpu_custom_call" | custom-call | flops 5368709120 | bytes 2359296 | tf_op jit(solution)/shard_map/pallas_call | solution.py:194
  42.8 0.0 collective-permute-done.7.refs_7_
  42.8 0.0 collective-permute-done.6.refs_6_
  42.8 6.3 %shard_map.93 = (f32[512,128]{1,0:T(8,128)S(1)}, bf16[512,128]{1,0:T(8,128)(2,1)S(1)}, bf16[512,128]{1,0:T(8,128)(2,1)S(1)}, bf16[512,128]{1,0:T(8,128)(2,1)S(1)...) custom-call(s32[14]{0:T(128)S(1)} %broadcast_select_fusion.table, ...), custom_call_target="tpu_custom_call" | custom-call | flops 3758096384 | bytes 3145728 | tf_op jit(solution)/shard_map/pallas_call | solution.py:194
  49.1 0.1 collective-permute-start.8
  49.2 2.7 %collective-permute-start.9 = (bf16[512,128]{1,0:T(8,128)(2,1)S(1)}, bf16[512,128]{1,0:T(8,128)(2,1)S(1)}, u32[]{:S(2)}, u32[]{:S(2)}) collective-permute-start(bf16[512,128]{1,0:T(8,128)(2,1)S(1)} %get-tuple-element.33), channel_id=1, source_target_pairs={{0,19},{8,72},{16,7},{24,88},{4,23},{12,76},{20,3},{28,92},{32,51}... | collective-permute-start | bytes 393224 | tf_op jit(solution)/shard_map/ppermute | solution.py:238
  51.8 2.9 %collective-permute-start.10 = (bf16[512,128]{1,0:T(8,128)(2,1)S(1)}, bf16[512,128]{1,0:T(8,128)(2,1)S(1)}, u32[]{:S(2)}, u32[]{:S(2)}) collective-permute-start(bf16[512,128]{1,0:T(8,128)(2,1)S(1)} %get-tuple-element.34), channel_id=1, source_target_pairs={{0,33},{8,28},{16,49},{24,8},{4,37},{12,24},{20,53},{28,12},{32,65... | collective-permute-start | bytes 393224 | tf_op jit(solution)/shard_map/ppermute | solution.py:238
  54.7 0.0 collective-permute-start.11
  54.7 1.0 %collective-permute-start.12 = (bf16[512,128]{1,0:T(8,128)(2,1)S(1)}, bf16[512,128]{1,0:T(8,128)(2,1)S(1)}, u32[]{:S(2)}, u32[]{:S(2)}) collective-permute-start(bf16[512,128]{1,0:T(8,128)(2,1)S(1)} %get-tuple-element.36), channel_id=1, source_target_pairs={{0,18},{8,73},{16,6},{24,89},{4,22},{12,77},{20,2},{28,93},{32,50}... | collective-permute-start | bytes 393224 | tf_op jit(solution)/shard_map/ppermute | solution.py:238
  55.7 0.0 collective-permute-done.8
  55.7 0.0 collective-permute-done.9
  55.7 0.9 %collective-permute-done.10 = bf16[512,128]{1,0:T(8,128)(2,1)S(1)} collective-permute-done((bf16[512,128]{1,0:T(8,128)(2,1)S(1)}, bf16[512,128]{1,0:T(8,128)(2,1)S(1)}, u32[]{:S(2)}, u32[]{:S(2)}) %collective-permute-start.10) | collective-permute-done | bytes 131104 | tf_op jit(solution)/shard_map/ppermute | solution.py:238
  56.7 6.7 %collective-permute-done.11 = bf16[512,128]{1,0:T(8,128)(2,1)S(1)} collective-permute-done((bf16[512,128]{1,0:T(8,128)(2,1)S(1)}, bf16[512,128]{1,0:T(8,128)(2,1)S(1)}, u32[]{:S(2)}, u32[]{:S(2)}) %collective-permute-start.11) | collective-permute-done | bytes 131104 | tf_op jit(solution)/shard_map/ppermute | solution.py:238
  63.3 0.0 collective-permute-done.12
  63.3 0.1 convert_add_fusion
  63.5 6.1 %collective-permute-start.13 = (f32[256,128]{1,0:T(8,128)S(1)}, f32[256,128]{1,0:T(8,128)S(1)}, u32[]{:S(2)}, u32[]{:S(2)}) collective-permute-start(f32[256,128]{1,0:T(8,128)S(1)} %slice.9), channel_id=1, source_target_pairs={{0,8},{8,0},{16,24},{24,16},{4,12},{12,4},{20,28},{28,20},{32,40},... | collective-permute-start | bytes 393224 | tf_op jit(solution)/shard_map/ppermute | solution.py:239
  69.6 1.0 %collective-permute-done.13 = f32[256,128]{1,0:T(8,128)S(1)} collective-permute-done((f32[256,128]{1,0:T(8,128)S(1)}, f32[256,128]{1,0:T(8,128)S(1)}, u32[]{:S(2)}, u32[]{:S(2)}) %collective-permute-start.13) | collective-permute-done | bytes 131104 | tf_op jit(solution)/shard_map/ppermute | solution.py:239
  70.6 0.7 slice_add_fusion
  (7 shorter events, 0.1 us)
Async XLA Ops:
  0.0 0.9 %copy-start = (bf16[256,128]{1,0:T(8,128)(2,1)S(1)}, bf16[256,128]{1,0:T(8,128)(2,1)}, u32[]{:S(2)}) copy-start(bf16[256,128]{1,0:T(8,128)(2,1)} %param.10) | copy-start | bytes 196612
  0.9 0.8 %copy-start.1 = (bf16[256,128]{1,0:T(8,128)(2,1)S(1)}, bf16[256,128]{1,0:T(8,128)(2,1)}, u32[]{:S(2)}) copy-start(bf16[256,128]{1,0:T(8,128)(2,1)} %param.11) | copy-start | bytes 196612
  1.8 2.6 %collective-permute-start = (bf16[256,384]{1,0:T(8,128)(2,1)S(1)}, bf16[256,384]{1,0:T(8,128)(2,1)S(1)}, u32[]{:S(2)}, u32[]{:S(2)}) collective-permute-start(bf16[256,384]{1,0:T(8,128)(2,1)S(1)} %constant_dynamic-update-slice_fusion), channel_id=1, source_target_pairs={{0,8},{8,0},{16,24},{24,16},{4,12},{12,4},{20,28},{28,20},{32,40},... | collective-permute-start | bytes 589832 | tf_op jit(solution)/shard_map/ppermute | solution.py:215
  3.3 8.9 %copy-start.6 = (s32[12]{0:T(128)S(1)}, s32[12]{0:T(128)}, u32[]{:S(2)}) copy-start(s32[12]{0:T(128)} %constant.33.clone) | copy-start | bytes 148
  3.3 8.9 %copy-start.7 = (s32[12]{0:T(128)S(1)}, s32[12]{0:T(128)}, u32[]{:S(2)}) copy-start(s32[12]{0:T(128)} %constant.32.clone) | copy-start | bytes 148
  4.4 7.9 %copy-start.4 = (s32[20]{0:T(128)S(1)}, s32[20]{0:T(128)}, u32[]{:S(2)}) copy-start(s32[20]{0:T(128)} %constant.35.clone) | copy-start | bytes 244
  4.4 7.9 %copy-start.5 = (s32[20]{0:T(128)S(1)}, s32[20]{0:T(128)}, u32[]{:S(2)}) copy-start(s32[20]{0:T(128)} %constant.34.clone) | copy-start | bytes 244
  4.4 9.3 %collective-permute-start.2 = (bf16[512,384]{1,0:T(8,128)(2,1)S(1)}, bf16[512,384]{1,0:T(8,128)(2,1)S(1)}, u32[]{:S(2)}, u32[]{:S(2)}) collective-permute-start(bf16[512,384]{1,0:T(8,128)(2,1)S(1)} %pad_maximum_fusion.refs_0_), channel_id=1, source_target_pairs={{19,0},{72,8},{7,16},{88,24},{23,4},{76,12},{3,20},{92,28},{51,32}... | collective-permute-start | bytes 1179656 | tf_op jit(solution)/shard_map/ppermute | solution.py:221
  7.5 11.5 %collective-permute-start.1 = (bf16[512,384]{1,0:T(8,128)(2,1)S(1)}, bf16[512,384]{1,0:T(8,128)(2,1)S(1)}, u32[]{:S(2)}, u32[]{:S(2)}) collective-permute-start(bf16[512,384]{1,0:T(8,128)(2,1)S(1)} %pad_maximum_fusion.refs_0_), channel_id=1, source_target_pairs={{116,0},{27,8},{96,16},{15,24},{112,4},{31,12},{100,20},{11,28},{2... | collective-permute-start | bytes 1179656 | tf_op jit(solution)/shard_map/ppermute | solution.py:221
  12.2 8.1 %copy-start.2 = (s32[14]{0:T(128)S(1)}, s32[14]{0:T(128)}, u32[]{:S(2)}) copy-start(s32[14]{0:T(128)} %constant.37.clone) | copy-start | bytes 172
  12.2 8.1 %copy-start.3 = (s32[14]{0:T(128)S(1)}, s32[14]{0:T(128)}, u32[]{:S(2)}) copy-start(s32[14]{0:T(128)} %constant.36.clone) | copy-start | bytes 172
  12.2 14.0 %collective-permute-start.3 = (bf16[512,384]{1,0:T(8,128)(2,1)S(1)}, bf16[512,384]{1,0:T(8,128)(2,1)S(1)}, u32[]{:S(2)}, u32[]{:S(2)}) collective-permute-start(bf16[512,384]{1,0:T(8,128)(2,1)S(1)} %pad_maximum_fusion.refs_0_), channel_id=1, source_target_pairs={{33,0},{28,8},{49,16},{8,24},{37,4},{24,12},{53,20},{12,28},{65,32... | collective-permute-start | bytes 1179656 | tf_op jit(solution)/shard_map/ppermute | solution.py:221
  13.7 18.7 %collective-permute-start.5 = (bf16[512,384]{1,0:T(8,128)(2,1)S(1)}, bf16[512,384]{1,0:T(8,128)(2,1)S(1)}, u32[]{:S(2)}, u32[]{:S(2)}) collective-permute-start(bf16[512,384]{1,0:T(8,128)(2,1)S(1)} %collective-permute-done.2.refs_2_.refs_3_), channel_id=1, source_target_pairs={{3,0},{9,8},{19,16},{25,24},{7,4},{13,12},{23,20},{29,28},{35,32},... | collective-permute-start | bytes 1179656 | tf_op jit(solution)/shard_map/ppermute | solution.py:221
  19.0 13.4 %collective-permute-start.4 = (bf16[512,384]{1,0:T(8,128)(2,1)S(1)}, bf16[512,384]{1,0:T(8,128)(2,1)S(1)}, u32[]{:S(2)}, u32[]{:S(2)}) collective-permute-start(bf16[512,384]{1,0:T(8,128)(2,1)S(1)} %collective-permute-done.1.refs_1_.refs_2_), channel_id=1, source_target_pairs={{4,0},{104,8},{20,16},{120,24},{0,4},{108,12},{16,20},{124,28},{36... | collective-permute-start | bytes 1179656 | tf_op jit(solution)/shard_map/ppermute | solution.py:221
  20.3 22.5 %collective-permute-start.7 = (bf16[512,384]{1,0:T(8,128)(2,1)S(1)}, bf16[512,384]{1,0:T(8,128)(2,1)S(1)}, u32[]{:S(2)}, u32[]{:S(2)}) collective-permute-start(bf16[512,384]{1,0:T(8,128)(2,1)S(1)} %collective-permute-done.1.refs_1_.refs_2_), channel_id=1, source_target_pairs={{32,0},{31,8},{48,16},{11,24},{36,4},{27,12},{52,20},{15,28},{64,3... | collective-permute-start | bytes 1179656 | tf_op jit(solution)/shard_map/ppermute | solution.py:221
  21.2 21.6 %collective-permute-start.6 = (bf16[512,384]{1,0:T(8,128)(2,1)S(1)}, bf16[512,384]{1,0:T(8,128)(2,1)S(1)}, u32[]{:S(2)}, u32[]{:S(2)}) collective-permute-start(bf16[512,384]{1,0:T(8,128)(2,1)S(1)} %collective-permute-done.1.refs_1_.refs_2_), channel_id=1, source_target_pairs={{96,0},{25,8},{112,16},{13,24},{100,4},{29,12},{116,20},{9,28},{0,... | collective-permute-start | bytes 1179656 | tf_op jit(solution)/shard_map/ppermute | solution.py:221
  49.1 6.6 %collective-permute-start.8 = (bf16[512,128]{1,0:T(8,128)(2,1)S(1)}, bf16[512,128]{1,0:T(8,128)(2,1)S(1)}, u32[]{:S(2)}, u32[]{:S(2)}) collective-permute-start(bf16[512,128]{1,0:T(8,128)(2,1)S(1)} %get-tuple-element.32), channel_id=1, source_target_pairs={{0,116},{8,27},{16,96},{24,15},{4,112},{12,31},{20,100},{28,11},{3... | collective-permute-start | bytes 393224 | tf_op jit(solution)/shard_map/ppermute | solution.py:238
  49.2 6.5 %collective-permute-start.9 = (bf16[512,128]{1,0:T(8,128)(2,1)S(1)}, bf16[512,128]{1,0:T(8,128)(2,1)S(1)}, u32[]{:S(2)}, u32[]{:S(2)}) collective-permute-start(bf16[512,128]{1,0:T(8,128)(2,1)S(1)} %get-tuple-element.33), channel_id=1, source_target_pairs={{0,19},{8,72},{16,7},{24,88},{4,23},{12,76},{20,3},{28,92},{32,51}... | collective-permute-start | bytes 393224 | tf_op jit(solution)/shard_map/ppermute | solution.py:238
  51.8 4.8 %collective-permute-start.10 = (bf16[512,128]{1,0:T(8,128)(2,1)S(1)}, bf16[512,128]{1,0:T(8,128)(2,1)S(1)}, u32[]{:S(2)}, u32[]{:S(2)}) collective-permute-start(bf16[512,128]{1,0:T(8,128)(2,1)S(1)} %get-tuple-element.34), channel_id=1, source_target_pairs={{0,33},{8,28},{16,49},{24,8},{4,37},{12,24},{20,53},{28,12},{32,65... | collective-permute-start | bytes 393224 | tf_op jit(solution)/shard_map/ppermute | solution.py:238
  54.7 8.6 %collective-permute-start.11 = (bf16[512,128]{1,0:T(8,128)(2,1)S(1)}, bf16[512,128]{1,0:T(8,128)(2,1)S(1)}, u32[]{:S(2)}, u32[]{:S(2)}) collective-permute-start(bf16[512,128]{1,0:T(8,128)(2,1)S(1)} %get-tuple-element.35), channel_id=1, source_target_pairs={{0,112},{8,123},{16,100},{24,111},{4,116},{12,127},{20,96},{28,107... | collective-permute-start | bytes 393224 | tf_op jit(solution)/shard_map/ppermute | solution.py:238
  54.7 8.6 %collective-permute-start.12 = (bf16[512,128]{1,0:T(8,128)(2,1)S(1)}, bf16[512,128]{1,0:T(8,128)(2,1)S(1)}, u32[]{:S(2)}, u32[]{:S(2)}) collective-permute-start(bf16[512,128]{1,0:T(8,128)(2,1)S(1)} %get-tuple-element.36), channel_id=1, source_target_pairs={{0,18},{8,73},{16,6},{24,89},{4,22},{12,77},{20,2},{28,93},{32,50}... | collective-permute-start | bytes 393224 | tf_op jit(solution)/shard_map/ppermute | solution.py:238
  63.5 7.1 %collective-permute-start.13 = (f32[256,128]{1,0:T(8,128)S(1)}, f32[256,128]{1,0:T(8,128)S(1)}, u32[]{:S(2)}, u32[]{:S(2)}) collective-permute-start(f32[256,128]{1,0:T(8,128)S(1)} %slice.9), channel_id=1, source_target_pairs={{0,8},{8,0},{16,24},{24,16},{4,12},{12,4},{20,28},{28,20},{32,40},... | collective-permute-start | bytes 393224 | tf_op jit(solution)/shard_map/ppermute | solution.py:239

commit v3 on v2

--- a/solution.py
+++ b/solution.py
@@ -15,19 +15,18 @@
     ((0, 0, 0), (3, 3, 1), (3, 0, 1), (0, 2, 0), (0, 0, 3), (1, 2, 0), (0, 0, 2), (2, 0, 0)),
 )
 SOURCE = (0, 2, 0, 0, 0, 3, 2, 2)
-KEPT = (0, 1, 2, 3, 4, 5)
 STAGES = (
     (
-        (((0, 4), (2, 0)), ((2, 3), (3, 2), (3, 4), (4, 3))),
-        (((2, 0), (4, 3)), ((0, 3), (0, 4), (4, 0), (4, 2))),
+        (((2, 0), (2, 4), (3, 2), (3, 4)), ((0, 4), (4, 0))),
+        (((2, 0), (2, 3), (2, 4), (4, 0)), ((3, 0), (4, 3))),
     ),
     (
-        (((0, 5), (1, 0), (1, 4), (1, 5), (2, 5), (3, 1), (5, 3)), ((2, 1), (4, 5), (5, 4))),
-        (((0, 5), (1, 0), (1, 2), (1, 3), (1, 4), (4, 5), (5, 1)), ((2, 5), (5, 2))),
+        (((1, 0), (1, 5), (2, 5), (3, 1), (5, 3)), ((1, 6), (1, 7), (3, 6), (4, 5), (4, 7), (5, 0), (5, 4), (5, 6), (5, 7))),
+        (((0, 5), (1, 2), (1, 3), (1, 4), (5, 1)), ((1, 0), (1, 6), (2, 5), (2, 6), (2, 7), (3, 6), (3, 7), (5, 2), (5, 6))),
     ),
     (
-        ((), ((1, 6), (1, 7), (3, 6), (3, 7), (4, 7), (5, 6), (5, 7))),
-        ((), ((0, 7), (1, 6), (2, 6), (2, 7), (3, 6), (3, 7), (5, 6))),
+        ((), ((0, 5), (0, 6))),
+        ((), ((0, 1), (0, 6), (0, 7))),
     ),
 )
 ORDER = (2, 3, 4, 1, 5, 6, 7)
@@ -98,14 +97,14 @@
 
 def prepare(i, chunk_ref, stage, left_x, right_x, left_v, right_v, turned):
     chunk = chunk_ref[...]
-    rows = chunk.shape[0]
     x = chunk[:, :FEAT]
     wide = x.astype(jnp.float32)
-    norm = jnp.sum(wide * wide, axis=1, keepdims=True)
+    norm = jnp.broadcast_to(jnp.sum(wide * wide, axis=1, keepdims=True), wide.shape)
     high = norm.astype(jnp.bfloat16).astype(jnp.float32)
     middle = (norm - high).astype(jnp.bfloat16).astype(jnp.float32)
     low = norm - high - middle
-    lane = lax.broadcasted_iota(jnp.int32, (rows, FEAT), 1)
+    lane = lax.broadcasted_iota(jnp.int32, wide.shape, 1)
+    rows = wide.shape[0]
     if i in stage.lefts:
         tail = jnp.where(lane == 3, high, jnp.where(lane == 4, middle, jnp.where(lane == 5, low, 0.0)))
         left_x[i, :, :FEAT] = (wide * -2.0).astype(jnp.bfloat16)

time: 71.8 us -> 66.1 us (0.921)
  starting transfers between devices: 32.7 us -> 24.4 us
  waiting for transfers between devices: 12.9 us -> 16.3 us
    ppermute x7, waiting for transfers between devices: 3.22 us -> 11.1 us  [local(): chunks[i] = lax.ppermute(chunks[SOURCE[i]], AXES, shift(moves))]
    ppermute x1, starting transfers between devices: 6.11 us -> 0.09 us  [local(): return total[:HALF] + lax.ppermute(total[HALF:], AXES, sibling())]
    ppermute x5, waiting for transfers between devices: 7.64 us -> 2.75 us  [local(): lax.ppermute(sums[i], AXES, shift(moves, back=True)).astype(jnp.float32)]
    ppermute x7, starting transfers between devices: 18.5 us -> 15.3 us  [local(): chunks[i] = lax.ppermute(chunks[SOURCE[i]], AXES, shift(moves))]
    ppermute x5, starting transfers between devices: 6.61 us -> 7.59 us  [local(): lax.ppermute(sums[i], AXES, shift(moves, back=True)).astype(jnp.float32)]
  transfers between devices with their start and end apart: 14 -> 14, of which waited for: 6 -> 7; matrix products, arithmetic and copies ran while one was open for 0% -> 0% of each run, Pallas kernels for 23% -> 15%
where the time goes in v3:
time: 66.1 us; the launch traced here: 65.9 us
  starting transfers between devices  24.4 us (37%)
  Pallas kernels  22.4 us (34%)
  waiting for transfers between devices  16.3 us (25%)
  local copies, waits for them, and re-layouts  1.78 us (3%)
  other arithmetic  0.83 us (1%)
    pallas_call x3, Pallas kernels, sums_over_pairs(): pl.pallas_call(functools.partial(pair_kernel, stage, tuple(before)), out_...  22.4 us
    ppermute x7, starting transfers between devices, local(): chunks[i] = lax.ppermute(chunks[SOURCE[i]], AXES, shift(moves))  15.3 us
    ppermute x7, waiting for transfers between devices, local(): chunks[i] = lax.ppermute(chunks[SOURCE[i]], AXES, shift(moves))  11.1 us
    ppermute x5, starting transfers between devices, local(): lax.ppermute(sums[i], AXES, shift(moves, back=True)).astype(jnp.float32)  7.59 us
    ppermute x5, waiting for transfers between devices, local(): lax.ppermute(sums[i], AXES, shift(moves, back=True)).astype(jnp.float32)  2.75 us
    unnamed x18, local copies, waits for them, and re-layouts  1.75 us
    ppermute x1, starting transfers between devices, local(): lax.ppermute(mine, AXES, sibling())  1.5 us
    ppermute x1, waiting for transfers between devices, local(): return total[:HALF] + lax.ppermute(total[HALF:], AXES, sibling())  1.33 us
  transfers between devices with their start and end apart: 14, of which 7 were waited for; matrix products, arithmetic and copies ran while one was open for 0% of the time, Pallas kernels for 15%

profile of v3, /device:TPU:1, one launch (start us, length us, event | category | flops | bytes accessed | tf_op | source)
XLA Modules:
  0.0 65.9 jit_solution(6777739131306953428)
XLA Ops:
  0.0 0.0 copy-start
  0.0 0.9 %constant_dynamic-update-slice_fusion.2 = bf16[256,384]{1,0:T(8,128)(2,1)S(1)} fusion(bf16[256,128]{1,0:T(8,128)(2,1)} %param.9), kind=kLoop, calls=%fused_computation.5 | loop fusion | bytes 131072
  0.9 0.0 copy-done
  0.9 0.0 copy-start.1
  0.9 0.8 %copy-done.1 = bf16[256,128]{1,0:T(8,128)(2,1)S(1)} copy-done((bf16[256,128]{1,0:T(8,128)(2,1)S(1)}, bf16[256,128]{1,0:T(8,128)(2,1)}, u32[]{:S(2)}) %copy-start.1) | copy-done | bytes 65560
  1.8 1.5 %collective-permute-start = (bf16[256,384]{1,0:T(8,128)(2,1)S(1)}, bf16[256,384]{1,0:T(8,128)(2,1)S(1)}, u32[]{:S(2)}, u32[]{:S(2)}) collective-permute-start(bf16[256,384]{1,0:T(8,128)(2,1)S(1)} %constant_dynamic-update-slice_fusion), channel_id=1, source_target_pairs={{0,8},{8,0},{16,24},{24,16},{4,12},{12,4},{20,28},{28,20},{32,40},... | collective-permute-start | bytes 589832 | tf_op jit(solution)/shard_map/ppermute | solution.py:214
  3.3 0.0 copy-start.6
  3.3 0.0 copy-start.7
  3.3 1.1 %collective-permute-done = bf16[256,384]{1,0:T(8,128)(2,1)S(1)} collective-permute-done((bf16[256,384]{1,0:T(8,128)(2,1)S(1)}, bf16[256,384]{1,0:T(8,128)(2,1)S(1)}, u32[]{:S(2)}, u32[]{:S(2)}) %collective-permute-start) | collective-permute-done | bytes 196640 | tf_op jit(solution)/shard_map/ppermute | solution.py:214
  4.4 0.0 copy-start.4
  4.4 0.0 copy-start.5
  4.4 4.8 %collective-permute-start.1 = (bf16[512,384]{1,0:T(8,128)(2,1)S(1)}, bf16[512,384]{1,0:T(8,128)(2,1)S(1)}, u32[]{:S(2)}, u32[]{:S(2)}) collective-permute-start(bf16[512,384]{1,0:T(8,128)(2,1)S(1)} %pad_maximum_fusion.refs_0_), channel_id=1, source_target_pairs={{116,0},{27,8},{96,16},{15,24},{112,4},{31,12},{100,20},{11,28},{2... | collective-permute-start | bytes 1179656 | tf_op jit(solution)/shard_map/ppermute | solution.py:220
  9.2 2.9 %collective-permute-start.2 = (bf16[512,384]{1,0:T(8,128)(2,1)S(1)}, bf16[512,384]{1,0:T(8,128)(2,1)S(1)}, u32[]{:S(2)}, u32[]{:S(2)}) collective-permute-start(bf16[512,384]{1,0:T(8,128)(2,1)S(1)} %pad_maximum_fusion.refs_0_), channel_id=1, source_target_pairs={{19,0},{72,8},{7,16},{88,24},{23,4},{76,12},{3,20},{92,28},{51,32}... | collective-permute-start | bytes 1179656 | tf_op jit(solution)/shard_map/ppermute | solution.py:220
  12.2 0.0 copy-done.6
  12.2 0.0 copy-done.7
  12.2 0.0 copy-start.2
  12.2 0.0 copy-start.3
  12.2 0.1 collective-permute-start.3
  12.3 0.0 copy-done.4
  12.3 0.0 copy-done.5
  12.3 4.8 %collective-permute-done.1.refs_1_.refs_2_ = bf16[512,384]{1,0:T(8,128)(2,1)S(1)} collective-permute-done((bf16[512,384]{1,0:T(8,128)(2,1)S(1)}, bf16[512,384]{1,0:T(8,128)(2,1)S(1)}, u32[]{:S(2)}, u32[]{:S(2)}) %collective-permute-start.1) | collective-permute-done | bytes 393248 | tf_op jit(solution)/shard_map/ppermute | solution.py:220
  17.1 1.3 %collective-permute-start.4 = (bf16[512,384]{1,0:T(8,128)(2,1)S(1)}, bf16[512,384]{1,0:T(8,128)(2,1)S(1)}, u32[]{:S(2)}, u32[]{:S(2)}) collective-permute-start(bf16[512,384]{1,0:T(8,128)(2,1)S(1)} %collective-permute-done.1.refs_1_.refs_2_), channel_id=1, source_target_pairs={{4,0},{104,8},{20,16},{120,24},{0,4},{108,12},{16,20},{124,28},{36... | collective-permute-start | bytes 1179656 | tf_op jit(solution)/shard_map/ppermute | solution.py:220
  18.4 5.6 %collective-permute-start.6 = (bf16[512,384]{1,0:T(8,128)(2,1)S(1)}, bf16[512,384]{1,0:T(8,128)(2,1)S(1)}, u32[]{:S(2)}, u32[]{:S(2)}) collective-permute-start(bf16[512,384]{1,0:T(8,128)(2,1)S(1)} %collective-permute-done.1.refs_1_.refs_2_), channel_id=1, source_target_pairs={{96,0},{25,8},{112,16},{13,24},{100,4},{29,12},{116,20},{9,28},{0,... | collective-permute-start | bytes 1179656 | tf_op jit(solution)/shard_map/ppermute | solution.py:220
  24.0 0.0 collective-permute-start.7
  24.0 0.0 collective-permute-done.2.refs_2_.refs_3_
  24.0 0.6 collective-permute-start.5
  24.6 0.0 copy-done.2
  24.6 0.0 copy-done.3
  24.6 0.0 collective-permute-done.3.refs_3_.refs_4_
  24.6 6.7 %shard_map.91 = (f32[512,128]{1,0:T(8,128)S(1)}, f32[512,128]{1,0:T(8,128)S(1)}, f32[512,128]{1,0:T(8,128)S(1)}, f32[512,128]{1,0:T(8,128)S(1)}) custom-call(s32[12]{0:T(128)S(1)} %broadcast_select_fusion.2.table, bf16[512,384]{1,0:T(8,128)(2,1)S(1)} %pad_maximum_fusion.refs_0_, bf16[512,384]{1,0:T(8,128)(2,1)S(1)} %collective-permute-done.1.refs_1_.refs_2_, ...), custom_call_target="tpu_custom_call" | custom-call | flops 3221225472 | bytes 1572864 | tf_op jit(solution)/shard_map/pallas_call | solution.py:193
  31.2 0.0 collective-permute-done.4.refs_1_
  31.2 4.6 %collective-permute-done.5.refs_5_.refs_2_ = bf16[512,384]{1,0:T(8,128)(2,1)S(1)} collective-permute-done((bf16[512,384]{1,0:T(8,128)(2,1)S(1)}, bf16[512,384]{1,0:T(8,128)(2,1)S(1)}, u32[]{:S(2)}, u32[]{:S(2)}) %collective-permute-start.5) | collective-permute-done | bytes 393248 | tf_op jit(solution)/shard_map/ppermute | solution.py:220
  35.9 0.0 collective-permute-done.6.refs_6_.refs_3_
  35.9 1.7 %collective-permute-done.7.refs_7_.refs_4_ = bf16[512,384]{1,0:T(8,128)(2,1)S(1)} collective-permute-done((bf16[512,384]{1,0:T(8,128)(2,1)S(1)}, bf16[512,384]{1,0:T(8,128)(2,1)S(1)}, u32[]{:S(2)}, u32[]{:S(2)}) %collective-permute-start.7) | collective-permute-done | bytes 393248 | tf_op jit(solution)/shard_map/ppermute | solution.py:220
  37.5 12.6 %shard_map.92 = (f32[512,128]{1,0:T(8,128)S(1)}, bf16[512,128]{1,0:T(8,128)(2,1)S(1)}, bf16[512,128]{1,0:T(8,128)(2,1)S(1)}, bf16[512,128]{1,0:T(8,128)(2,1)S(1)...) custom-call(s32[28]{0:T(128)S(1)} %broadcast_select_fusion.1.table, ...), custom_call_target="tpu_custom_call" | custom-call | flops 7516192768 | bytes 3145728 | tf_op jit(solution)/shard_map/pallas_call | solution.py:193
  50.1 1.6 %collective-permute-start.12 = (bf16[512,128]{1,0:T(8,128)(2,1)S(1)}, bf16[512,128]{1,0:T(8,128)(2,1)S(1)}, u32[]{:S(2)}, u32[]{:S(2)}) collective-permute-start(bf16[512,128]{1,0:T(8,128)(2,1)S(1)} %get-tuple-element.24), channel_id=1, source_target_pairs={{0,18},{8,73},{16,6},{24,89},{4,22},{12,77},{20,2},{28,93},{32,50}... | collective-permute-start | bytes 393224 | tf_op jit(solution)/shard_map/ppermute | solution.py:237
  51.8 0.0 collective-permute-start.11
  51.8 5.2 %collective-permute-start.10 = (bf16[512,128]{1,0:T(8,128)(2,1)S(1)}, bf16[512,128]{1,0:T(8,128)(2,1)S(1)}, u32[]{:S(2)}, u32[]{:S(2)}) collective-permute-start(bf16[512,128]{1,0:T(8,128)(2,1)S(1)} %get-tuple-element.22), channel_id=1, source_target_pairs={{0,33},{8,28},{16,49},{24,8},{4,37},{12,24},{20,53},{28,12},{32,65... | collective-permute-start | bytes 393224 | tf_op jit(solution)/shard_map/ppermute | solution.py:237
  56.9 0.8 %collective-permute-start.9 = (bf16[512,128]{1,0:T(8,128)(2,1)S(1)}, bf16[512,128]{1,0:T(8,128)(2,1)S(1)}, u32[]{:S(2)}, u32[]{:S(2)}) collective-permute-start(bf16[512,128]{1,0:T(8,128)(2,1)S(1)} %get-tuple-element.21), channel_id=1, source_target_pairs={{0,19},{8,72},{16,7},{24,88},{4,23},{12,76},{20,3},{28,92},{32,51}... | collective-permute-start | bytes 393224 | tf_op jit(solution)/shard_map/ppermute | solution.py:237
  57.7 0.0 collective-permute-start.8
  57.7 3.1 %shard_map.93 = f32[512,128]{1,0:T(8,128)S(1)} custom-call(s32[6]{0:T(128)S(1)} %broadcast_select_fusion.table, bf16[512,384]{1,0:T(8,128)(2,1)S(1)} %pad_maximum_fusion.refs_0_, bf16[512,384]{1,0:T(8,128)(2,1)S(1)} %collective-permute-done.4.refs_1_, bf16[512,384]{1,0:T(8,128)(2,1)S(1)} %collective-permute-done.5.refs_5_.refs_2_, ...), custom_call_target="tpu_custom_call" | custom-call | flops 1610612736 | bytes 1966080 | tf_op jit(solution)/shard_map/pallas_call | solution.py:193
  60.9 0.0 collective-permute-done.12
  60.9 0.0 collective-permute-done.11
  60.9 0.0 collective-permute-done.10
  60.9 1.3 %collective-permute-done.9 = bf16[512,128]{1,0:T(8,128)(2,1)S(1)} collective-permute-done((bf16[512,128]{1,0:T(8,128)(2,1)S(1)}, bf16[512,128]{1,0:T(8,128)(2,1)S(1)}, u32[]{:S(2)}, u32[]{:S(2)}) %collective-permute-start.9) | collective-permute-done | bytes 131104 | tf_op jit(solution)/shard_map/ppermute | solution.py:237
  62.2 1.4 %collective-permute-done.8 = bf16[512,128]{1,0:T(8,128)(2,1)S(1)} collective-permute-done((bf16[512,128]{1,0:T(8,128)(2,1)S(1)}, bf16[512,128]{1,0:T(8,128)(2,1)S(1)}, u32[]{:S(2)}, u32[]{:S(2)}) %collective-permute-start.8) | collective-permute-done | bytes 131104 | tf_op jit(solution)/shard_map/ppermute | solution.py:237
  63.7 0.1 convert_add_fusion
  63.8 0.1 collective-permute-start.13
  63.9 1.3 %collective-permute-done.13 = f32[256,128]{1,0:T(8,128)S(1)} collective-permute-done((f32[256,128]{1,0:T(8,128)S(1)}, f32[256,128]{1,0:T(8,128)S(1)}, u32[]{:S(2)}, u32[]{:S(2)}) %collective-permute-start.13) | collective-permute-done | bytes 131104 | tf_op jit(solution)/shard_map/ppermute | solution.py:238
  65.2 0.7 %slice_add_fusion = f32[256,128]{1,0:T(8,128)} fusion(f32[256,128]{1,0:T(8,128)S(1)} %collective-permute-done.13, f32[512,128]{1,0:T(8,128)S(1)} %convert_add_fusion), kind=kLoop, calls=%fused_computation.2 | loop fusion | flops 32768 | bytes 393216 | tf_op jit(solution)/shard_map/add | solution.py:238
  (7 shorter events, 0.1 us)
Async XLA Ops:
  0.0 0.9 %copy-start = (bf16[256,128]{1,0:T(8,128)(2,1)S(1)}, bf16[256,128]{1,0:T(8,128)(2,1)}, u32[]{:S(2)}) copy-start(bf16[256,128]{1,0:T(8,128)(2,1)} %param.10) | copy-start | bytes 196612
  0.9 0.8 %copy-start.1 = (bf16[256,128]{1,0:T(8,128)(2,1)S(1)}, bf16[256,128]{1,0:T(8,128)(2,1)}, u32[]{:S(2)}) copy-start(bf16[256,128]{1,0:T(8,128)(2,1)} %param.11) | copy-start | bytes 196612
  1.8 2.6 %collective-permute-start = (bf16[256,384]{1,0:T(8,128)(2,1)S(1)}, bf16[256,384]{1,0:T(8,128)(2,1)S(1)}, u32[]{:S(2)}, u32[]{:S(2)}) collective-permute-start(bf16[256,384]{1,0:T(8,128)(2,1)S(1)} %constant_dynamic-update-slice_fusion), channel_id=1, source_target_pairs={{0,8},{8,0},{16,24},{24,16},{4,12},{12,4},{20,28},{28,20},{32,40},... | collective-permute-start | bytes 589832 | tf_op jit(solution)/shard_map/ppermute | solution.py:214
  3.3 8.9 %copy-start.6 = (s32[28]{0:T(128)S(1)}, s32[28]{0:T(128)}, u32[]{:S(2)}) copy-start(s32[28]{0:T(128)} %constant.34.clone) | copy-start | bytes 340
  3.3 8.9 %copy-start.7 = (s32[28]{0:T(128)S(1)}, s32[28]{0:T(128)}, u32[]{:S(2)}) copy-start(s32[28]{0:T(128)} %constant.35.clone) | copy-start | bytes 340
  4.4 7.9 %copy-start.4 = (s32[12]{0:T(128)S(1)}, s32[12]{0:T(128)}, u32[]{:S(2)}) copy-start(s32[12]{0:T(128)} %constant.32.clone) | copy-start | bytes 148
  4.4 7.9 %copy-start.5 = (s32[12]{0:T(128)S(1)}, s32[12]{0:T(128)}, u32[]{:S(2)}) copy-start(s32[12]{0:T(128)} %constant.33.clone) | copy-start | bytes 148
  4.4 12.7 %collective-permute-start.1 = (bf16[512,384]{1,0:T(8,128)(2,1)S(1)}, bf16[512,384]{1,0:T(8,128)(2,1)S(1)}, u32[]{:S(2)}, u32[]{:S(2)}) collective-permute-start(bf16[512,384]{1,0:T(8,128)(2,1)S(1)} %pad_maximum_fusion.refs_0_), channel_id=1, source_target_pairs={{116,0},{27,8},{96,16},{15,24},{112,4},{31,12},{100,20},{11,28},{2... | collective-permute-start | bytes 1179656 | tf_op jit(solution)/shard_map/ppermute | solution.py:220
  9.2 14.8 %collective-permute-start.2 = (bf16[512,384]{1,0:T(8,128)(2,1)S(1)}, bf16[512,384]{1,0:T(8,128)(2,1)S(1)}, u32[]{:S(2)}, u32[]{:S(2)}) collective-permute-start(bf16[512,384]{1,0:T(8,128)(2,1)S(1)} %pad_maximum_fusion.refs_0_), channel_id=1, source_target_pairs={{19,0},{72,8},{7,16},{88,24},{23,4},{76,12},{3,20},{92,28},{51,32}... | collective-permute-start | bytes 1179656 | tf_op jit(solution)/shard_map/ppermute | solution.py:220
  12.2 12.4 %copy-start.2 = (s32[6]{0:T(128)S(1)}, s32[6]{0:T(128)}, u32[]{:S(2)}) copy-start(s32[6]{0:T(128)} %constant.36.clone) | copy-start | bytes 76
  12.2 12.4 %copy-start.3 = (s32[6]{0:T(128)S(1)}, s32[6]{0:T(128)}, u32[]{:S(2)}) copy-start(s32[6]{0:T(128)} %constant.37.clone) | copy-start | bytes 76
  12.2 12.4 %collective-permute-start.3 = (bf16[512,384]{1,0:T(8,128)(2,1)S(1)}, bf16[512,384]{1,0:T(8,128)(2,1)S(1)}, u32[]{:S(2)}, u32[]{:S(2)}) collective-permute-start(bf16[512,384]{1,0:T(8,128)(2,1)S(1)} %pad_maximum_fusion.refs_0_), channel_id=1, source_target_pairs={{33,0},{28,8},{49,16},{8,24},{37,4},{24,12},{53,20},{12,28},{65,32... | collective-permute-start | bytes 1179656 | tf_op jit(solution)/shard_map/ppermute | solution.py:220
  17.1 14.1 %collective-permute-start.4 = (bf16[512,384]{1,0:T(8,128)(2,1)S(1)}, bf16[512,384]{1,0:T(8,128)(2,1)S(1)}, u32[]{:S(2)}, u32[]{:S(2)}) collective-permute-start(bf16[512,384]{1,0:T(8,128)(2,1)S(1)} %collective-permute-done.1.refs_1_.refs_2_), channel_id=1, source_target_pairs={{4,0},{104,8},{20,16},{120,24},{0,4},{108,12},{16,20},{124,28},{36... | collective-permute-start | bytes 1179656 | tf_op jit(solution)/shard_map/ppermute | solution.py:220
  18.4 17.5 %collective-permute-start.6 = (bf16[512,384]{1,0:T(8,128)(2,1)S(1)}, bf16[512,384]{1,0:T(8,128)(2,1)S(1)}, u32[]{:S(2)}, u32[]{:S(2)}) collective-permute-start(bf16[512,384]{1,0:T(8,128)(2,1)S(1)} %collective-permute-done.1.refs_1_.refs_2_), channel_id=1, source_target_pairs={{96,0},{25,8},{112,16},{13,24},{100,4},{29,12},{116,20},{9,28},{0,... | collective-permute-start | bytes 1179656 | tf_op jit(solution)/shard_map/ppermute | solution.py:220
  24.0 13.5 %collective-permute-start.7 = (bf16[512,384]{1,0:T(8,128)(2,1)S(1)}, bf16[512,384]{1,0:T(8,128)(2,1)S(1)}, u32[]{:S(2)}, u32[]{:S(2)}) collective-permute-start(bf16[512,384]{1,0:T(8,128)(2,1)S(1)} %collective-permute-done.1.refs_1_.refs_2_), channel_id=1, source_target_pairs={{32,0},{31,8},{48,16},{11,24},{36,4},{27,12},{52,20},{15,28},{64,3... | collective-permute-start | bytes 1179656 | tf_op jit(solution)/shard_map/ppermute | solution.py:220
  24.0 11.9 %collective-permute-start.5 = (bf16[512,384]{1,0:T(8,128)(2,1)S(1)}, bf16[512,384]{1,0:T(8,128)(2,1)S(1)}, u32[]{:S(2)}, u32[]{:S(2)}) collective-permute-start(bf16[512,384]{1,0:T(8,128)(2,1)S(1)} %collective-permute-done.2.refs_2_.refs_3_), channel_id=1, source_target_pairs={{3,0},{9,8},{19,16},{25,24},{7,4},{13,12},{23,20},{29,28},{35,32},... | collective-permute-start | bytes 1179656 | tf_op jit(solution)/shard_map/ppermute | solution.py:220
  50.1 10.7 %collective-permute-start.12 = (bf16[512,128]{1,0:T(8,128)(2,1)S(1)}, bf16[512,128]{1,0:T(8,128)(2,1)S(1)}, u32[]{:S(2)}, u32[]{:S(2)}) collective-permute-start(bf16[512,128]{1,0:T(8,128)(2,1)S(1)} %get-tuple-element.24), channel_id=1, source_target_pairs={{0,18},{8,73},{16,6},{24,89},{4,22},{12,77},{20,2},{28,93},{32,50}... | collective-permute-start | bytes 393224 | tf_op jit(solution)/shard_map/ppermute | solution.py:237
  51.8 9.1 %collective-permute-start.11 = (bf16[512,128]{1,0:T(8,128)(2,1)S(1)}, bf16[512,128]{1,0:T(8,128)(2,1)S(1)}, u32[]{:S(2)}, u32[]{:S(2)}) collective-permute-start(bf16[512,128]{1,0:T(8,128)(2,1)S(1)} %get-tuple-element.23), channel_id=1, source_target_pairs={{0,112},{8,123},{16,100},{24,111},{4,116},{12,127},{20,96},{28,107... | collective-permute-start | bytes 393224 | tf_op jit(solution)/shard_map/ppermute | solution.py:237
  51.8 9.1 %collective-permute-start.10 = (bf16[512,128]{1,0:T(8,128)(2,1)S(1)}, bf16[512,128]{1,0:T(8,128)(2,1)S(1)}, u32[]{:S(2)}, u32[]{:S(2)}) collective-permute-start(bf16[512,128]{1,0:T(8,128)(2,1)S(1)} %get-tuple-element.22), channel_id=1, source_target_pairs={{0,33},{8,28},{16,49},{24,8},{4,37},{12,24},{20,53},{28,12},{32,65... | collective-permute-start | bytes 393224 | tf_op jit(solution)/shard_map/ppermute | solution.py:237
  56.9 5.3 %collective-permute-start.9 = (bf16[512,128]{1,0:T(8,128)(2,1)S(1)}, bf16[512,128]{1,0:T(8,128)(2,1)S(1)}, u32[]{:S(2)}, u32[]{:S(2)}) collective-permute-start(bf16[512,128]{1,0:T(8,128)(2,1)S(1)} %get-tuple-element.21), channel_id=1, source_target_pairs={{0,19},{8,72},{16,7},{24,88},{4,23},{12,76},{20,3},{28,92},{32,51}... | collective-permute-start | bytes 393224 | tf_op jit(solution)/shard_map/ppermute | solution.py:237
  57.7 5.9 %collective-permute-start.8 = (bf16[512,128]{1,0:T(8,128)(2,1)S(1)}, bf16[512,128]{1,0:T(8,128)(2,1)S(1)}, u32[]{:S(2)}, u32[]{:S(2)}) collective-permute-start(bf16[512,128]{1,0:T(8,128)(2,1)S(1)} %get-tuple-element.20), channel_id=1, source_target_pairs={{0,116},{8,27},{16,96},{24,15},{4,112},{12,31},{20,100},{28,11},{3... | collective-permute-start | bytes 393224 | tf_op jit(solution)/shard_map/ppermute | solution.py:237
  63.8 1.4 %collective-permute-start.13 = (f32[256,128]{1,0:T(8,128)S(1)}, f32[256,128]{1,0:T(8,128)S(1)}, u32[]{:S(2)}, u32[]{:S(2)}) collective-permute-start(f32[256,128]{1,0:T(8,128)S(1)} %slice.9), channel_id=1, source_target_pairs={{0,8},{8,0},{16,24},{24,16},{4,12},{12,4},{20,28},{28,20},{32,40},... | collective-permute-start | bytes 393224 | tf_op jit(solution)/shard_map/ppermute | solution.py:238

commit v4 on v3

--- a/solution.py
+++ b/solution.py
@@ -184,6 +184,21 @@
         out_ref[...] = grad.astype(out_ref.dtype)
 
 
+def side_by_side(x_ref, left_ref, right_ref, out_ref):
+    for n, ref in enumerate((x_ref, left_ref, right_ref)):
+        out_ref[:, n * FEAT : (n + 1) * FEAT] = ref[...]
+
+
+def joined(x, left, right):
+    whole = pl.BlockSpec(memory_space=pltpu.VMEM)
+    return pl.pallas_call(
+        side_by_side,
+        out_shape=jax.ShapeDtypeStruct((x.shape[0], 3 * FEAT), x.dtype),
+        in_specs=[whole] * 3,
+        out_specs=whole,
+    )(x, left, right)
+
+
 def sums_over_pairs(stage, table, chunks, before, kinds):
     whole = pl.BlockSpec(memory_space=pltpu.VMEM)
     stack = pltpu.VMEM((stage.slots, ROWS, 2 * FEAT), jnp.bfloat16)
@@ -210,7 +225,7 @@
 
 def local(features, left_vectors, right_vectors):
     core = lax.axis_index("blk") % 2
-    mine = jnp.concatenate([features, left_vectors, right_vectors], axis=1)
+    mine = joined(features, left_vectors, right_vectors)
     chunks = [jnp.concatenate([mine, lax.ppermute(mine, AXES, sibling())], axis=0)]
     chunks += [None] * (HELD - 1)
     for i in ORDER:

time: 66.1 us -> 66.9 us (1.012)
  local copies, waits for them, and re-layouts: 1.78 us -> 0.05 us
  Pallas kernels: 22.4 us -> 24 us
  other arithmetic: 0.83 us -> 1.77 us
    unnamed x18 -> x12, local copies, waits for them, and re-layouts: 1.75 us -> 0.03 us
    pallas_call x0 -> x1, Pallas kernels: none -> 1.6 us  [joined(): pl.pallas_call(side_by_side, out_shape=jax.ShapeDtypeStruct((x.shape[0],...]
    concatenate x1, other arithmetic: 0.04 us -> 0.97 us  [local(): jnp.concatenate([mine, lax.ppermute(mine, AXES, sibling())], axis=0)]
where the time goes in v4:
time: 66.9 us; the launch traced here: 66.8 us
  starting transfers between devices  24.3 us (36%)
  Pallas kernels  24 us (36%)
  waiting for transfers between devices  16.5 us (25%)
  other arithmetic  1.77 us (3%)
    pallas_call x3, Pallas kernels, sums_over_pairs(): pl.pallas_call(functools.partial(pair_kernel, stage, tuple(before)), out_...  22.4 us
    ppermute x7, starting transfers between devices, local(): chunks[i] = lax.ppermute(chunks[SOURCE[i]], AXES, shift(moves))  15.3 us
    ppermute x7, waiting for transfers between devices, local(): chunks[i] = lax.ppermute(chunks[SOURCE[i]], AXES, shift(moves))  11.1 us
    ppermute x5, starting transfers between devices, local(): lax.ppermute(sums[i], AXES, shift(moves, back=True)).astype(jnp.float32)  7.59 us
    ppermute x5, waiting for transfers between devices, local(): lax.ppermute(sums[i], AXES, shift(moves, back=True)).astype(jnp.float32)  2.76 us
    pallas_call x1, Pallas kernels, joined(): pl.pallas_call(side_by_side, out_shape=jax.ShapeDtypeStruct((x.shape[0],...  1.6 us
    ppermute x1, starting transfers between devices, local(): lax.ppermute(mine, AXES, sibling())  1.42 us
  transfers between devices with their start and end apart: 14, of which 7 were waited for; matrix products, arithmetic and copies ran while one was open for 0% of the time, Pallas kernels for 15%

profile of v4, /device:TPU:1, one launch (start us, length us, event | category | flops | bytes accessed | tf_op | source)
XLA Modules:
  0.0 66.8 jit_solution(611346830356835590)
XLA Ops:
  0.0 1.6 %shard_map.91 = bf16[256,384]{1,0:T(8,128)(2,1)} custom-call(bf16[256,128]{1,0:T(8,128)(2,1)} %x_ref.1, bf16[256,128]{1,0:T(8,128)(2,1)} %left_ref.1, bf16[256,128]{1,0:T(8,128)(2,1)} %right_ref.1), custom_call_target="tpu_custom_call" | custom-call | tf_op jit(solution)/shard_map/pallas_call | solution.py:194
  1.6 1.4 %collective-permute-start = (bf16[256,384]{1,0:T(8,128)(2,1)}, bf16[256,384]{1,0:T(8,128)(2,1)S(1)}, u32[]{:S(2)}, u32[]{:S(2)}) collective-permute-start(bf16[256,384]{1,0:T(8,128)(2,1)} %shard_map.91), channel_id=1, source_target_pairs={{0,8},{8,0},{16,24},{24,16},{4,12},{12,4},{20,28},{28,20},{32,40},... | collective-permute-start | bytes 589832 | tf_op jit(solution)/shard_map/ppermute | solution.py:229
  3.0 0.0 copy-start.4
  3.0 0.0 copy-start.5
  3.0 1.3 %collective-permute-done = bf16[256,384]{1,0:T(8,128)(2,1)S(1)} collective-permute-done((bf16[256,384]{1,0:T(8,128)(2,1)}, bf16[256,384]{1,0:T(8,128)(2,1)S(1)}, u32[]{:S(2)}, u32[]{:S(2)}) %collective-permute-start) | collective-permute-done | bytes 196640 | tf_op jit(solution)/shard_map/ppermute | solution.py:229
  4.3 1.0 %pad_maximum_fusion.refs_0_ = bf16[512,384]{1,0:T(8,128)(2,1)S(1)} fusion(bf16[256,384]{1,0:T(8,128)(2,1)S(1)} %collective-permute-done, bf16[256,384]{1,0:T(8,128)(2,1)} %shard_map.91), kind=kLoop, calls=%fused_computation | loop fusion | flops 786432 | bytes 786432 | tf_op jit(solution)/shard_map/concatenate | solution.py:229
  5.3 0.0 copy-start.2
  5.3 0.0 copy-start.3
  5.3 4.8 %collective-permute-start.1 = (bf16[512,384]{1,0:T(8,128)(2,1)S(1)}, bf16[512,384]{1,0:T(8,128)(2,1)S(1)}, u32[]{:S(2)}, u32[]{:S(2)}) collective-permute-start(bf16[512,384]{1,0:T(8,128)(2,1)S(1)} %pad_maximum_fusion.refs_0_), channel_id=1, source_target_pairs={{116,0},{27,8},{96,16},{15,24},{112,4},{31,12},{100,20},{11,28},{2... | collective-permute-start | bytes 1179656 | tf_op jit(solution)/shard_map/ppermute | solution.py:235
  10.1 2.9 %collective-permute-start.2 = (bf16[512,384]{1,0:T(8,128)(2,1)S(1)}, bf16[512,384]{1,0:T(8,128)(2,1)S(1)}, u32[]{:S(2)}, u32[]{:S(2)}) collective-permute-start(bf16[512,384]{1,0:T(8,128)(2,1)S(1)} %pad_maximum_fusion.refs_0_), channel_id=1, source_target_pairs={{19,0},{72,8},{7,16},{88,24},{23,4},{76,12},{3,20},{92,28},{51,32}... | collective-permute-start | bytes 1179656 | tf_op jit(solution)/shard_map/ppermute | solution.py:235
  13.0 0.0 copy-done.4
  13.1 0.0 copy-done.5
  13.1 0.0 copy-start
  13.1 0.0 copy-start.1
  13.1 0.1 collective-permute-start.3
  13.2 0.0 copy-done.2
  13.2 0.0 copy-done.3
  13.2 4.8 %collective-permute-done.1.refs_1_.refs_2_ = bf16[512,384]{1,0:T(8,128)(2,1)S(1)} collective-permute-done((bf16[512,384]{1,0:T(8,128)(2,1)S(1)}, bf16[512,384]{1,0:T(8,128)(2,1)S(1)}, u32[]{:S(2)}, u32[]{:S(2)}) %collective-permute-start.1) | collective-permute-done | bytes 393248 | tf_op jit(solution)/shard_map/ppermute | solution.py:235
  18.0 1.3 %collective-permute-start.4 = (bf16[512,384]{1,0:T(8,128)(2,1)S(1)}, bf16[512,384]{1,0:T(8,128)(2,1)S(1)}, u32[]{:S(2)}, u32[]{:S(2)}) collective-permute-start(bf16[512,384]{1,0:T(8,128)(2,1)S(1)} %collective-permute-done.1.refs_1_.refs_2_), channel_id=1, source_target_pairs={{4,0},{104,8},{20,16},{120,24},{0,4},{108,12},{16,20},{124,28},{36... | collective-permute-start | bytes 1179656 | tf_op jit(solution)/shard_map/ppermute | solution.py:235
  19.3 5.6 %collective-permute-start.6 = (bf16[512,384]{1,0:T(8,128)(2,1)S(1)}, bf16[512,384]{1,0:T(8,128)(2,1)S(1)}, u32[]{:S(2)}, u32[]{:S(2)}) collective-permute-start(bf16[512,384]{1,0:T(8,128)(2,1)S(1)} %collective-permute-done.1.refs_1_.refs_2_), channel_id=1, source_target_pairs={{96,0},{25,8},{112,16},{13,24},{100,4},{29,12},{116,20},{9,28},{0,... | collective-permute-start | bytes 1179656 | tf_op jit(solution)/shard_map/ppermute | solution.py:235
  24.9 0.0 collective-permute-start.7
  24.9 0.0 collective-permute-done.2.refs_2_.refs_3_
  24.9 0.6 collective-permute-start.5
  25.4 0.0 copy-done
  25.5 0.0 copy-done.1
  25.5 0.0 collective-permute-done.3.refs_3_.refs_4_
  25.5 6.6 %shard_map.92 = (f32[512,128]{1,0:T(8,128)S(1)}, f32[512,128]{1,0:T(8,128)S(1)}, f32[512,128]{1,0:T(8,128)S(1)}, f32[512,128]{1,0:T(8,128)S(1)}) custom-call(s32[12]{0:T(128)S(1)} %broadcast_select_fusion.2.table, bf16[512,384]{1,0:T(8,128)(2,1)S(1)} %pad_maximum_fusion.refs_0_, bf16[512,384]{1,0:T(8,128)(2,1)S(1)} %collective-permute-done.1.refs_1_.refs_2_, ...), custom_call_target="tpu_custom_call" | custom-call | flops 3221225472 | bytes 1572864 | tf_op jit(solution)/shard_map/pallas_call | solution.py:208
  32.1 0.0 collective-permute-done.4.refs_1_
  32.1 4.6 %collective-permute-done.5.refs_5_.refs_2_ = bf16[512,384]{1,0:T(8,128)(2,1)S(1)} collective-permute-done((bf16[512,384]{1,0:T(8,128)(2,1)S(1)}, bf16[512,384]{1,0:T(8,128)(2,1)S(1)}, u32[]{:S(2)}, u32[]{:S(2)}) %collective-permute-start.5) | collective-permute-done | bytes 393248 | tf_op jit(solution)/shard_map/ppermute | solution.py:235
  36.8 0.0 collective-permute-done.6.refs_6_.refs_3_
  36.8 1.6 %collective-permute-done.7.refs_7_.refs_4_ = bf16[512,384]{1,0:T(8,128)(2,1)S(1)} collective-permute-done((bf16[512,384]{1,0:T(8,128)(2,1)S(1)}, bf16[512,384]{1,0:T(8,128)(2,1)S(1)}, u32[]{:S(2)}, u32[]{:S(2)}) %collective-permute-start.7) | collective-permute-done | bytes 393248 | tf_op jit(solution)/shard_map/ppermute | solution.py:235
  38.4 12.6 %shard_map.93 = (f32[512,128]{1,0:T(8,128)S(1)}, bf16[512,128]{1,0:T(8,128)(2,1)S(1)}, bf16[512,128]{1,0:T(8,128)(2,1)S(1)}, bf16[512,128]{1,0:T(8,128)(2,1)S(1)...) custom-call(s32[28]{0:T(128)S(1)} %broadcast_select_fusion.1.table, ...), custom_call_target="tpu_custom_call" | custom-call | flops 7516192768 | bytes 3145728 | tf_op jit(solution)/shard_map/pallas_call | solution.py:208
  51.0 1.6 %collective-permute-start.12 = (bf16[512,128]{1,0:T(8,128)(2,1)S(1)}, bf16[512,128]{1,0:T(8,128)(2,1)S(1)}, u32[]{:S(2)}, u32[]{:S(2)}) collective-permute-start(bf16[512,128]{1,0:T(8,128)(2,1)S(1)} %get-tuple-element.24), channel_id=1, source_target_pairs={{0,18},{8,73},{16,6},{24,89},{4,22},{12,77},{20,2},{28,93},{32,50}... | collective-permute-start | bytes 393224 | tf_op jit(solution)/shard_map/ppermute | solution.py:252
  52.6 0.0 collective-permute-start.11
  52.6 5.2 %collective-permute-start.10 = (bf16[512,128]{1,0:T(8,128)(2,1)S(1)}, bf16[512,128]{1,0:T(8,128)(2,1)S(1)}, u32[]{:S(2)}, u32[]{:S(2)}) collective-permute-start(bf16[512,128]{1,0:T(8,128)(2,1)S(1)} %get-tuple-element.22), channel_id=1, source_target_pairs={{0,33},{8,28},{16,49},{24,8},{4,37},{12,24},{20,53},{28,12},{32,65... | collective-permute-start | bytes 393224 | tf_op jit(solution)/shard_map/ppermute | solution.py:252
  57.8 0.8 %collective-permute-start.9 = (bf16[512,128]{1,0:T(8,128)(2,1)S(1)}, bf16[512,128]{1,0:T(8,128)(2,1)S(1)}, u32[]{:S(2)}, u32[]{:S(2)}) collective-permute-start(bf16[512,128]{1,0:T(8,128)(2,1)S(1)} %get-tuple-element.21), channel_id=1, source_target_pairs={{0,19},{8,72},{16,7},{24,88},{4,23},{12,76},{20,3},{28,92},{32,51}... | collective-permute-start | bytes 393224 | tf_op jit(solution)/shard_map/ppermute | solution.py:252
  58.6 0.0 collective-permute-start.8
  58.6 3.1 %shard_map.94 = f32[512,128]{1,0:T(8,128)S(1)} custom-call(s32[6]{0:T(128)S(1)} %broadcast_select_fusion.table, bf16[512,384]{1,0:T(8,128)(2,1)S(1)} %pad_maximum_fusion.refs_0_, bf16[512,384]{1,0:T(8,128)(2,1)S(1)} %collective-permute-done.4.refs_1_, bf16[512,384]{1,0:T(8,128)(2,1)S(1)} %collective-permute-done.5.refs_5_.refs_2_, ...), custom_call_target="tpu_custom_call" | custom-call | flops 1610612736 | bytes 1966080 | tf_op jit(solution)/shard_map/pallas_call | solution.py:208
  61.7 0.0 collective-permute-done.12
  61.7 0.0 collective-permute-done.11
  61.7 0.0 collective-permute-done.10
  61.8 1.3 %collective-permute-done.9 = bf16[512,128]{1,0:T(8,128)(2,1)S(1)} collective-permute-done((bf16[512,128]{1,0:T(8,128)(2,1)S(1)}, bf16[512,128]{1,0:T(8,128)(2,1)S(1)}, u32[]{:S(2)}, u32[]{:S(2)}) %collective-permute-start.9) | collective-permute-done | bytes 131104 | tf_op jit(solution)/shard_map/ppermute | solution.py:252
  63.1 1.4 %collective-permute-done.8 = bf16[512,128]{1,0:T(8,128)(2,1)S(1)} collective-permute-done((bf16[512,128]{1,0:T(8,128)(2,1)S(1)}, bf16[512,128]{1,0:T(8,128)(2,1)S(1)}, u32[]{:S(2)}, u32[]{:S(2)}) %collective-permute-start.8) | collective-permute-done | bytes 131104 | tf_op jit(solution)/shard_map/ppermute | solution.py:252
  64.5 0.1 convert_add_fusion
  64.6 0.1 collective-permute-start.13
  64.7 1.3 %collective-permute-done.13 = f32[256,128]{1,0:T(8,128)S(1)} collective-permute-done((f32[256,128]{1,0:T(8,128)S(1)}, f32[256,128]{1,0:T(8,128)S(1)}, u32[]{:S(2)}, u32[]{:S(2)}) %collective-permute-start.13) | collective-permute-done | bytes 131104 | tf_op jit(solution)/shard_map/ppermute | solution.py:253
  66.1 0.7 %slice_add_fusion = f32[256,128]{1,0:T(8,128)} fusion(f32[256,128]{1,0:T(8,128)S(1)} %collective-permute-done.13, f32[512,128]{1,0:T(8,128)S(1)} %convert_add_fusion), kind=kLoop, calls=%fused_computation.2 | loop fusion | flops 32768 | bytes 393216 | tf_op jit(solution)/shard_map/add | solution.py:253
  (4 shorter events, 0.0 us)
Async XLA Ops:
  1.6 2.7 %collective-permute-start = (bf16[256,384]{1,0:T(8,128)(2,1)}, bf16[256,384]{1,0:T(8,128)(2,1)S(1)}, u32[]{:S(2)}, u32[]{:S(2)}) collective-permute-start(bf16[256,384]{1,0:T(8,128)(2,1)} %shard_map.91), channel_id=1, source_target_pairs={{0,8},{8,0},{16,24},{24,16},{4,12},{12,4},{20,28},{28,20},{32,40},... | collective-permute-start | bytes 589832 | tf_op jit(solution)/shard_map/ppermute | solution.py:229
  3.0 10.0 %copy-start.4 = (s32[28]{0:T(128)S(1)}, s32[28]{0:T(128)}, u32[]{:S(2)}) copy-start(s32[28]{0:T(128)} %constant.34.clone) | copy-start | bytes 340
  3.0 10.0 %copy-start.5 = (s32[28]{0:T(128)S(1)}, s32[28]{0:T(128)}, u32[]{:S(2)}) copy-start(s32[28]{0:T(128)} %constant.35.clone) | copy-start | bytes 340
  5.3 7.9 %copy-start.2 = (s32[12]{0:T(128)S(1)}, s32[12]{0:T(128)}, u32[]{:S(2)}) copy-start(s32[12]{0:T(128)} %constant.32.clone) | copy-start | bytes 148
  5.3 7.9 %copy-start.3 = (s32[12]{0:T(128)S(1)}, s32[12]{0:T(128)}, u32[]{:S(2)}) copy-start(s32[12]{0:T(128)} %constant.33.clone) | copy-start | bytes 148
  5.3 12.7 %collective-permute-start.1 = (bf16[512,384]{1,0:T(8,128)(2,1)S(1)}, bf16[512,384]{1,0:T(8,128)(2,1)S(1)}, u32[]{:S(2)}, u32[]{:S(2)}) collective-permute-start(bf16[512,384]{1,0:T(8,128)(2,1)S(1)} %pad_maximum_fusion.refs_0_), channel_id=1, source_target_pairs={{116,0},{27,8},{96,16},{15,24},{112,4},{31,12},{100,20},{11,28},{2... | collective-permute-start | bytes 1179656 | tf_op jit(solution)/shard_map/ppermute | solution.py:235
  10.1 14.8 %collective-permute-start.2 = (bf16[512,384]{1,0:T(8,128)(2,1)S(1)}, bf16[512,384]{1,0:T(8,128)(2,1)S(1)}, u32[]{:S(2)}, u32[]{:S(2)}) collective-permute-start(bf16[512,384]{1,0:T(8,128)(2,1)S(1)} %pad_maximum_fusion.refs_0_), channel_id=1, source_target_pairs={{19,0},{72,8},{7,16},{88,24},{23,4},{76,12},{3,20},{92,28},{51,32}... | collective-permute-start | bytes 1179656 | tf_op jit(solution)/shard_map/ppermute | solution.py:235
  13.1 12.4 %copy-start = (s32[6]{0:T(128)S(1)}, s32[6]{0:T(128)}, u32[]{:S(2)}) copy-start(s32[6]{0:T(128)} %constant.36.clone) | copy-start | bytes 76
  13.1 12.4 %copy-start.1 = (s32[6]{0:T(128)S(1)}, s32[6]{0:T(128)}, u32[]{:S(2)}) copy-start(s32[6]{0:T(128)} %constant.37.clone) | copy-start | bytes 76
  13.1 12.4 %collective-permute-start.3 = (bf16[512,384]{1,0:T(8,128)(2,1)S(1)}, bf16[512,384]{1,0:T(8,128)(2,1)S(1)}, u32[]{:S(2)}, u32[]{:S(2)}) collective-permute-start(bf16[512,384]{1,0:T(8,128)(2,1)S(1)} %pad_maximum_fusion.refs_0_), channel_id=1, source_target_pairs={{33,0},{28,8},{49,16},{8,24},{37,4},{24,12},{53,20},{12,28},{65,32... | collective-permute-start | bytes 1179656 | tf_op jit(solution)/shard_map/ppermute | solution.py:235
  18.0 14.1 %collective-permute-start.4 = (bf16[512,384]{1,0:T(8,128)(2,1)S(1)}, bf16[512,384]{1,0:T(8,128)(2,1)S(1)}, u32[]{:S(2)}, u32[]{:S(2)}) collective-permute-start(bf16[512,384]{1,0:T(8,128)(2,1)S(1)} %collective-permute-done.1.refs_1_.refs_2_), channel_id=1, source_target_pairs={{4,0},{104,8},{20,16},{120,24},{0,4},{108,12},{16,20},{124,28},{36... | collective-permute-start | bytes 1179656 | tf_op jit(solution)/shard_map/ppermute | solution.py:235
  19.3 17.5 %collective-permute-start.6 = (bf16[512,384]{1,0:T(8,128)(2,1)S(1)}, bf16[512,384]{1,0:T(8,128)(2,1)S(1)}, u32[]{:S(2)}, u32[]{:S(2)}) collective-permute-start(bf16[512,384]{1,0:T(8,128)(2,1)S(1)} %collective-permute-done.1.refs_1_.refs_2_), channel_id=1, source_target_pairs={{96,0},{25,8},{112,16},{13,24},{100,4},{29,12},{116,20},{9,28},{0,... | collective-permute-start | bytes 1179656 | tf_op jit(solution)/shard_map/ppermute | solution.py:235
  24.9 13.5 %collective-permute-start.7 = (bf16[512,384]{1,0:T(8,128)(2,1)S(1)}, bf16[512,384]{1,0:T(8,128)(2,1)S(1)}, u32[]{:S(2)}, u32[]{:S(2)}) collective-permute-start(bf16[512,384]{1,0:T(8,128)(2,1)S(1)} %collective-permute-done.1.refs_1_.refs_2_), channel_id=1, source_target_pairs={{32,0},{31,8},{48,16},{11,24},{36,4},{27,12},{52,20},{15,28},{64,3... | collective-permute-start | bytes 1179656 | tf_op jit(solution)/shard_map/ppermute | solution.py:235
  24.9 11.9 %collective-permute-start.5 = (bf16[512,384]{1,0:T(8,128)(2,1)S(1)}, bf16[512,384]{1,0:T(8,128)(2,1)S(1)}, u32[]{:S(2)}, u32[]{:S(2)}) collective-permute-start(bf16[512,384]{1,0:T(8,128)(2,1)S(1)} %collective-permute-done.2.refs_2_.refs_3_), channel_id=1, source_target_pairs={{3,0},{9,8},{19,16},{25,24},{7,4},{13,12},{23,20},{29,28},{35,32},... | collective-permute-start | bytes 1179656 | tf_op jit(solution)/shard_map/ppermute | solution.py:235
  51.0 10.7 %collective-permute-start.12 = (bf16[512,128]{1,0:T(8,128)(2,1)S(1)}, bf16[512,128]{1,0:T(8,128)(2,1)S(1)}, u32[]{:S(2)}, u32[]{:S(2)}) collective-permute-start(bf16[512,128]{1,0:T(8,128)(2,1)S(1)} %get-tuple-element.24), channel_id=1, source_target_pairs={{0,18},{8,73},{16,6},{24,89},{4,22},{12,77},{20,2},{28,93},{32,50}... | collective-permute-start | bytes 393224 | tf_op jit(solution)/shard_map/ppermute | solution.py:252
  52.6 9.1 %collective-permute-start.11 = (bf16[512,128]{1,0:T(8,128)(2,1)S(1)}, bf16[512,128]{1,0:T(8,128)(2,1)S(1)}, u32[]{:S(2)}, u32[]{:S(2)}) collective-permute-start(bf16[512,128]{1,0:T(8,128)(2,1)S(1)} %get-tuple-element.23), channel_id=1, source_target_pairs={{0,112},{8,123},{16,100},{24,111},{4,116},{12,127},{20,96},{28,107... | collective-permute-start | bytes 393224 | tf_op jit(solution)/shard_map/ppermute | solution.py:252
  52.6 9.1 %collective-permute-start.10 = (bf16[512,128]{1,0:T(8,128)(2,1)S(1)}, bf16[512,128]{1,0:T(8,128)(2,1)S(1)}, u32[]{:S(2)}, u32[]{:S(2)}) collective-permute-start(bf16[512,128]{1,0:T(8,128)(2,1)S(1)} %get-tuple-element.22), channel_id=1, source_target_pairs={{0,33},{8,28},{16,49},{24,8},{4,37},{12,24},{20,53},{28,12},{32,65... | collective-permute-start | bytes 393224 | tf_op jit(solution)/shard_map/ppermute | solution.py:252
  57.8 5.3 %collective-permute-start.9 = (bf16[512,128]{1,0:T(8,128)(2,1)S(1)}, bf16[512,128]{1,0:T(8,128)(2,1)S(1)}, u32[]{:S(2)}, u32[]{:S(2)}) collective-permute-start(bf16[512,128]{1,0:T(8,128)(2,1)S(1)} %get-tuple-element.21), channel_id=1, source_target_pairs={{0,19},{8,72},{16,7},{24,88},{4,23},{12,76},{20,3},{28,92},{32,51}... | collective-permute-start | bytes 393224 | tf_op jit(solution)/shard_map/ppermute | solution.py:252
  58.6 5.9 %collective-permute-start.8 = (bf16[512,128]{1,0:T(8,128)(2,1)S(1)}, bf16[512,128]{1,0:T(8,128)(2,1)S(1)}, u32[]{:S(2)}, u32[]{:S(2)}) collective-permute-start(bf16[512,128]{1,0:T(8,128)(2,1)S(1)} %get-tuple-element.20), channel_id=1, source_target_pairs={{0,116},{8,27},{16,96},{24,15},{4,112},{12,31},{20,100},{28,11},{3... | collective-permute-start | bytes 393224 | tf_op jit(solution)/shard_map/ppermute | solution.py:252
  64.6 1.4 %collective-permute-start.13 = (f32[256,128]{1,0:T(8,128)S(1)}, f32[256,128]{1,0:T(8,128)S(1)}, u32[]{:S(2)}, u32[]{:S(2)}) collective-permute-start(f32[256,128]{1,0:T(8,128)S(1)} %slice.9), channel_id=1, source_target_pairs={{0,8},{8,0},{16,24},{24,16},{4,12},{12,4},{20,28},{28,20},{32,40},... | collective-permute-start | bytes 393224 | tf_op jit(solution)/shard_map/ppermute | solution.py:253

commit v5 on v3

--- a/solution.py
+++ b/solution.py
@@ -11,8 +11,8 @@
 from jax.sharding import PartitionSpec as P
 
 MEMBERS = (
-    ((0, 0, 0), (0, 3, 1), (0, 3, 3), (3, 0, 1), (1, 1, 0), (2, 0, 1), (0, 2, 3), (0, 0, 3)),
-    ((0, 0, 0), (3, 3, 1), (3, 0, 1), (0, 2, 0), (0, 0, 3), (1, 2, 0), (0, 0, 2), (2, 0, 0)),
+    ((0, 0, 0), (1, 3, 0), (3, 3, 0), (1, 0, 3), (0, 1, 1), (1, 0, 2), (3, 2, 0), (3, 0, 0)),
+    ((0, 0, 0), (1, 3, 3), (1, 0, 3), (0, 2, 0), (3, 0, 0), (0, 2, 1), (2, 0, 0), (0, 0, 2)),
 )
 SOURCE = (0, 2, 0, 0, 0, 3, 2, 2)
 STAGES = (

time: 66.1 us -> 66.6 us (level)
  starting transfers between devices: 24.4 us -> 25.3 us
    ppermute x5, starting transfers between devices: 7.59 us -> 9.71 us  [local(): lax.ppermute(sums[i], AXES, shift(moves, back=True)).astype(jnp.float32)]
    ppermute x7, starting transfers between devices: 15.3 us -> 14 us  [local(): chunks[i] = lax.ppermute(chunks[SOURCE[i]], AXES, shift(moves))]
where the time goes in v5:
time: 66.6 us; the launch traced here: 66.5 us
  starting transfers between devices  25.3 us (38%)
  Pallas kernels  22.4 us (34%)
  waiting for transfers between devices  16 us (24%)
  local copies, waits for them, and re-layouts  1.78 us (3%)
  other arithmetic  0.83 us (1%)
    pallas_call x3, Pallas kernels, sums_over_pairs(): pl.pallas_call(functools.partial(pair_kernel, stage, tuple(before)), out_...  22.4 us
    ppermute x7, starting transfers between devices, local(): chunks[i] = lax.ppermute(chunks[SOURCE[i]], AXES, shift(moves))  14 us
    ppermute x7, waiting for transfers between devices, local(): chunks[i] = lax.ppermute(chunks[SOURCE[i]], AXES, shift(moves))  10.8 us
    ppermute x5, starting transfers between devices, local(): lax.ppermute(sums[i], AXES, shift(moves, back=True)).astype(jnp.float32)  9.71 us
    ppermute x5, waiting for transfers between devices, local(): lax.ppermute(sums[i], AXES, shift(moves, back=True)).astype(jnp.float32)  2.75 us
    unnamed x18, local copies, waits for them, and re-layouts  1.75 us
    ppermute x1, starting transfers between devices, local(): lax.ppermute(mine, AXES, sibling())  1.5 us
    ppermute x1, waiting for transfers between devices, local(): return total[:HALF] + lax.ppermute(total[HALF:], AXES, sibling())  1.33 us
  transfers between devices with their start and end apart: 14, of which 7 were waited for; matrix products, arithmetic and copies ran while one was open for 0% of the time, Pallas kernels for 15%

profile of v5, /device:TPU:1, one launch (start us, length us, event | category | flops | bytes accessed | tf_op | source)
XLA Modules:
  0.0 66.5 jit_solution(1648604101334124507)
XLA Ops:
  0.0 0.0 copy-start
  0.0 0.9 %constant_dynamic-update-slice_fusion.2 = bf16[256,384]{1,0:T(8,128)(2,1)S(1)} fusion(bf16[256,128]{1,0:T(8,128)(2,1)} %param.9), kind=kLoop, calls=%fused_computation.5 | loop fusion | bytes 131072
  0.9 0.0 copy-done
  0.9 0.0 copy-start.1
  0.9 0.8 %copy-done.1 = bf16[256,128]{1,0:T(8,128)(2,1)S(1)} copy-done((bf16[256,128]{1,0:T(8,128)(2,1)S(1)}, bf16[256,128]{1,0:T(8,128)(2,1)}, u32[]{:S(2)}) %copy-start.1) | copy-done | bytes 65560
  1.8 1.5 %collective-permute-start = (bf16[256,384]{1,0:T(8,128)(2,1)S(1)}, bf16[256,384]{1,0:T(8,128)(2,1)S(1)}, u32[]{:S(2)}, u32[]{:S(2)}) collective-permute-start(bf16[256,384]{1,0:T(8,128)(2,1)S(1)} %constant_dynamic-update-slice_fusion), channel_id=1, source_target_pairs={{0,8},{8,0},{16,24},{24,16},{4,12},{12,4},{20,28},{28,20},{32,40},... | collective-permute-start | bytes 589832 | tf_op jit(solution)/shard_map/ppermute | solution.py:214
  3.3 0.0 copy-start.6
  3.3 0.0 copy-start.7
  3.3 1.1 %collective-permute-done = bf16[256,384]{1,0:T(8,128)(2,1)S(1)} collective-permute-done((bf16[256,384]{1,0:T(8,128)(2,1)S(1)}, bf16[256,384]{1,0:T(8,128)(2,1)S(1)}, u32[]{:S(2)}, u32[]{:S(2)}) %collective-permute-start) | collective-permute-done | bytes 196640 | tf_op jit(solution)/shard_map/ppermute | solution.py:214
  4.4 0.0 copy-start.4
  4.4 0.0 copy-start.5
  4.4 4.0 %collective-permute-start.1 = (bf16[512,384]{1,0:T(8,128)(2,1)S(1)}, bf16[512,384]{1,0:T(8,128)(2,1)S(1)}, u32[]{:S(2)}, u32[]{:S(2)}) collective-permute-start(bf16[512,384]{1,0:T(8,128)(2,1)S(1)} %pad_maximum_fusion.refs_0_), channel_id=1, source_target_pairs={{99,0},{29,8},{115,16},{9,24},{103,4},{25,12},{119,20},{13,28},{3,... | collective-permute-start | bytes 1179656 | tf_op jit(solution)/shard_map/ppermute | solution.py:220
  8.4 2.9 %collective-permute-start.2 = (bf16[512,384]{1,0:T(8,128)(2,1)S(1)}, bf16[512,384]{1,0:T(8,128)(2,1)S(1)}, u32[]{:S(2)}, u32[]{:S(2)}) collective-permute-start(bf16[512,384]{1,0:T(8,128)(2,1)S(1)} %pad_maximum_fusion.refs_0_), channel_id=1, source_target_pairs={{21,0},{72,8},{1,16},{88,24},{17,4},{76,12},{5,20},{92,28},{53,32}... | collective-permute-start | bytes 1179656 | tf_op jit(solution)/shard_map/ppermute | solution.py:220
  11.3 0.0 copy-done.6
  11.3 0.0 copy-done.7
  11.3 0.0 copy-start.2
  11.3 0.0 copy-start.3
  11.3 0.1 collective-permute-start.3
  11.4 0.0 copy-done.4
  11.4 0.0 copy-done.5
  11.5 4.3 %collective-permute-done.1.refs_1_.refs_2_ = bf16[512,384]{1,0:T(8,128)(2,1)S(1)} collective-permute-done((bf16[512,384]{1,0:T(8,128)(2,1)S(1)}, bf16[512,384]{1,0:T(8,128)(2,1)S(1)}, u32[]{:S(2)}, u32[]{:S(2)}) %collective-permute-start.1) | collective-permute-done | bytes 393248 | tf_op jit(solution)/shard_map/ppermute | solution.py:220
  15.8 1.3 %collective-permute-start.4 = (bf16[512,384]{1,0:T(8,128)(2,1)S(1)}, bf16[512,384]{1,0:T(8,128)(2,1)S(1)}, u32[]{:S(2)}, u32[]{:S(2)}) collective-permute-start(bf16[512,384]{1,0:T(8,128)(2,1)S(1)} %collective-permute-done.1.refs_1_.refs_2_), channel_id=1, source_target_pairs={{2,0},{104,8},{18,16},{120,24},{6,4},{108,12},{22,20},{124,28},{34... | collective-permute-start | bytes 1179656 | tf_op jit(solution)/shard_map/ppermute | solution.py:220
  17.1 5.6 %collective-permute-start.6 = (bf16[512,384]{1,0:T(8,128)(2,1)S(1)}, bf16[512,384]{1,0:T(8,128)(2,1)S(1)}, u32[]{:S(2)}, u32[]{:S(2)}) collective-permute-start(bf16[512,384]{1,0:T(8,128)(2,1)S(1)} %collective-permute-done.1.refs_1_.refs_2_), channel_id=1, source_target_pairs={{96,0},{25,8},{112,16},{13,24},{100,4},{29,12},{116,20},{9,28},{0,... | collective-permute-start | bytes 1179656 | tf_op jit(solution)/shard_map/ppermute | solution.py:220
  22.7 0.0 collective-permute-start.7
  22.7 0.0 collective-permute-done.2.refs_2_.refs_3_
  22.7 0.1 collective-permute-start.5
  22.8 0.0 copy-done.2
  22.8 0.0 copy-done.3
  22.8 0.0 collective-permute-done.3.refs_3_.refs_4_
  22.8 6.7 %shard_map.91 = (f32[512,128]{1,0:T(8,128)S(1)}, f32[512,128]{1,0:T(8,128)S(1)}, f32[512,128]{1,0:T(8,128)S(1)}, f32[512,128]{1,0:T(8,128)S(1)}) custom-call(s32[12]{0:T(128)S(1)} %broadcast_select_fusion.2.table, bf16[512,384]{1,0:T(8,128)(2,1)S(1)} %pad_maximum_fusion.refs_0_, bf16[512,384]{1,0:T(8,128)(2,1)S(1)} %collective-permute-done.1.refs_1_.refs_2_, ...), custom_call_target="tpu_custom_call" | custom-call | flops 3221225472 | bytes 1572864 | tf_op jit(solution)/shard_map/pallas_call | solution.py:193
  29.5 0.0 collective-permute-done.4.refs_1_
  29.5 1.2 %collective-permute-done.5.refs_5_.refs_2_ = bf16[512,384]{1,0:T(8,128)(2,1)S(1)} collective-permute-done((bf16[512,384]{1,0:T(8,128)(2,1)S(1)}, bf16[512,384]{1,0:T(8,128)(2,1)S(1)}, u32[]{:S(2)}, u32[]{:S(2)}) %collective-permute-start.5) | collective-permute-done | bytes 393248 | tf_op jit(solution)/shard_map/ppermute | solution.py:220
  30.7 0.3 collective-permute-done.6.refs_6_.refs_3_
  31.0 4.9 %collective-permute-done.7.refs_7_.refs_4_ = bf16[512,384]{1,0:T(8,128)(2,1)S(1)} collective-permute-done((bf16[512,384]{1,0:T(8,128)(2,1)S(1)}, bf16[512,384]{1,0:T(8,128)(2,1)S(1)}, u32[]{:S(2)}, u32[]{:S(2)}) %collective-permute-start.7) | collective-permute-done | bytes 393248 | tf_op jit(solution)/shard_map/ppermute | solution.py:220
  36.0 12.6 %shard_map.92 = (f32[512,128]{1,0:T(8,128)S(1)}, bf16[512,128]{1,0:T(8,128)(2,1)S(1)}, bf16[512,128]{1,0:T(8,128)(2,1)S(1)}, bf16[512,128]{1,0:T(8,128)(2,1)S(1)...) custom-call(s32[28]{0:T(128)S(1)} %broadcast_select_fusion.1.table, ...), custom_call_target="tpu_custom_call" | custom-call | flops 7516192768 | bytes 3145728 | tf_op jit(solution)/shard_map/pallas_call | solution.py:193
  48.6 0.1 collective-permute-start.12
  48.7 2.8 %collective-permute-start.11 = (bf16[512,128]{1,0:T(8,128)(2,1)S(1)}, bf16[512,128]{1,0:T(8,128)(2,1)S(1)}, u32[]{:S(2)}, u32[]{:S(2)}) collective-permute-start(bf16[512,128]{1,0:T(8,128)(2,1)S(1)} %get-tuple-element.23), channel_id=1, source_target_pairs={{0,97},{8,125},{16,113},{24,105},{4,101},{12,121},{20,117},{28,109... | collective-permute-start | bytes 393224 | tf_op jit(solution)/shard_map/ppermute | solution.py:237
  51.4 4.0 %collective-permute-start.10 = (bf16[512,128]{1,0:T(8,128)(2,1)S(1)}, bf16[512,128]{1,0:T(8,128)(2,1)S(1)}, u32[]{:S(2)}, u32[]{:S(2)}) collective-permute-start(bf16[512,128]{1,0:T(8,128)(2,1)S(1)} %get-tuple-element.22), channel_id=1, source_target_pairs={{0,48},{8,11},{16,36},{24,27},{4,52},{12,15},{20,32},{28,31},{32,8... | collective-permute-start | bytes 393224 | tf_op jit(solution)/shard_map/ppermute | solution.py:237
  55.5 2.8 %collective-permute-start.9 = (bf16[512,128]{1,0:T(8,128)(2,1)S(1)}, bf16[512,128]{1,0:T(8,128)(2,1)S(1)}, u32[]{:S(2)}, u32[]{:S(2)}) collective-permute-start(bf16[512,128]{1,0:T(8,128)(2,1)S(1)} %get-tuple-element.21), channel_id=1, source_target_pairs={{0,21},{8,72},{16,1},{24,88},{4,17},{12,76},{20,5},{28,92},{32,53}... | collective-permute-start | bytes 393224 | tf_op jit(solution)/shard_map/ppermute | solution.py:237
  58.3 0.0 collective-permute-start.8
  58.3 3.1 %shard_map.93 = f32[512,128]{1,0:T(8,128)S(1)} custom-call(s32[6]{0:T(128)S(1)} %broadcast_select_fusion.table, bf16[512,384]{1,0:T(8,128)(2,1)S(1)} %pad_maximum_fusion.refs_0_, bf16[512,384]{1,0:T(8,128)(2,1)S(1)} %collective-permute-done.4.refs_1_, bf16[512,384]{1,0:T(8,128)(2,1)S(1)} %collective-permute-done.5.refs_5_.refs_2_, ...), custom_call_target="tpu_custom_call" | custom-call | flops 1610612736 | bytes 1966080 | tf_op jit(solution)/shard_map/pallas_call | solution.py:193
  61.5 0.0 collective-permute-done.12
  61.5 0.0 collective-permute-done.11
  61.5 0.0 collective-permute-done.10
  61.5 0.0 collective-permute-done.9
  61.5 2.7 %collective-permute-done.8 = bf16[512,128]{1,0:T(8,128)(2,1)S(1)} collective-permute-done((bf16[512,128]{1,0:T(8,128)(2,1)S(1)}, bf16[512,128]{1,0:T(8,128)(2,1)S(1)}, u32[]{:S(2)}, u32[]{:S(2)}) %collective-permute-start.8) | collective-permute-done | bytes 131104 | tf_op jit(solution)/shard_map/ppermute | solution.py:237
  64.2 0.1 convert_add_fusion
  64.4 0.1 collective-permute-start.13
  64.5 1.3 %collective-permute-done.13 = f32[256,128]{1,0:T(8,128)S(1)} collective-permute-done((f32[256,128]{1,0:T(8,128)S(1)}, f32[256,128]{1,0:T(8,128)S(1)}, u32[]{:S(2)}, u32[]{:S(2)}) %collective-permute-start.13) | collective-permute-done | bytes 131104 | tf_op jit(solution)/shard_map/ppermute | solution.py:238
  65.8 0.7 %slice_add_fusion = f32[256,128]{1,0:T(8,128)} fusion(f32[256,128]{1,0:T(8,128)S(1)} %collective-permute-done.13, f32[512,128]{1,0:T(8,128)S(1)} %convert_add_fusion), kind=kLoop, calls=%fused_computation.2 | loop fusion | flops 32768 | bytes 393216 | tf_op jit(solution)/shard_map/add | solution.py:238
  (7 shorter events, 0.1 us)
Async XLA Ops:
  0.0 0.9 %copy-start = (bf16[256,128]{1,0:T(8,128)(2,1)S(1)}, bf16[256,128]{1,0:T(8,128)(2,1)}, u32[]{:S(2)}) copy-start(bf16[256,128]{1,0:T(8,128)(2,1)} %param.10) | copy-start | bytes 196612
  0.9 0.8 %copy-start.1 = (bf16[256,128]{1,0:T(8,128)(2,1)S(1)}, bf16[256,128]{1,0:T(8,128)(2,1)}, u32[]{:S(2)}) copy-start(bf16[256,128]{1,0:T(8,128)(2,1)} %param.11) | copy-start | bytes 196612
  1.8 2.6 %collective-permute-start = (bf16[256,384]{1,0:T(8,128)(2,1)S(1)}, bf16[256,384]{1,0:T(8,128)(2,1)S(1)}, u32[]{:S(2)}, u32[]{:S(2)}) collective-permute-start(bf16[256,384]{1,0:T(8,128)(2,1)S(1)} %constant_dynamic-update-slice_fusion), channel_id=1, source_target_pairs={{0,8},{8,0},{16,24},{24,16},{4,12},{12,4},{20,28},{28,20},{32,40},... | collective-permute-start | bytes 589832 | tf_op jit(solution)/shard_map/ppermute | solution.py:214
  3.3 8.0 %copy-start.6 = (s32[28]{0:T(128)S(1)}, s32[28]{0:T(128)}, u32[]{:S(2)}) copy-start(s32[28]{0:T(128)} %constant.34.clone) | copy-start | bytes 340
  3.3 8.0 %copy-start.7 = (s32[28]{0:T(128)S(1)}, s32[28]{0:T(128)}, u32[]{:S(2)}) copy-start(s32[28]{0:T(128)} %constant.35.clone) | copy-start | bytes 340
  4.4 7.0 %copy-start.4 = (s32[12]{0:T(128)S(1)}, s32[12]{0:T(128)}, u32[]{:S(2)}) copy-start(s32[12]{0:T(128)} %constant.32.clone) | copy-start | bytes 148
  4.4 7.0 %copy-start.5 = (s32[12]{0:T(128)S(1)}, s32[12]{0:T(128)}, u32[]{:S(2)}) copy-start(s32[12]{0:T(128)} %constant.33.clone) | copy-start | bytes 148
  4.4 11.4 %collective-permute-start.1 = (bf16[512,384]{1,0:T(8,128)(2,1)S(1)}, bf16[512,384]{1,0:T(8,128)(2,1)S(1)}, u32[]{:S(2)}, u32[]{:S(2)}) collective-permute-start(bf16[512,384]{1,0:T(8,128)(2,1)S(1)} %pad_maximum_fusion.refs_0_), channel_id=1, source_target_pairs={{99,0},{29,8},{115,16},{9,24},{103,4},{25,12},{119,20},{13,28},{3,... | collective-permute-start | bytes 1179656 | tf_op jit(solution)/shard_map/ppermute | solution.py:220
  8.4 14.3 %collective-permute-start.2 = (bf16[512,384]{1,0:T(8,128)(2,1)S(1)}, bf16[512,384]{1,0:T(8,128)(2,1)S(1)}, u32[]{:S(2)}, u32[]{:S(2)}) collective-permute-start(bf16[512,384]{1,0:T(8,128)(2,1)S(1)} %pad_maximum_fusion.refs_0_), channel_id=1, source_target_pairs={{21,0},{72,8},{1,16},{88,24},{17,4},{76,12},{5,20},{92,28},{53,32}... | collective-permute-start | bytes 1179656 | tf_op jit(solution)/shard_map/ppermute | solution.py:220
  11.3 11.5 %copy-start.2 = (s32[6]{0:T(128)S(1)}, s32[6]{0:T(128)}, u32[]{:S(2)}) copy-start(s32[6]{0:T(128)} %constant.36.clone) | copy-start | bytes 76
  11.3 11.5 %copy-start.3 = (s32[6]{0:T(128)S(1)}, s32[6]{0:T(128)}, u32[]{:S(2)}) copy-start(s32[6]{0:T(128)} %constant.37.clone) | copy-start | bytes 76
  11.3 11.5 %collective-permute-start.3 = (bf16[512,384]{1,0:T(8,128)(2,1)S(1)}, bf16[512,384]{1,0:T(8,128)(2,1)S(1)}, u32[]{:S(2)}, u32[]{:S(2)}) collective-permute-start(bf16[512,384]{1,0:T(8,128)(2,1)S(1)} %pad_maximum_fusion.refs_0_), channel_id=1, source_target_pairs={{48,0},{11,8},{36,16},{27,24},{52,4},{15,12},{32,20},{31,28},{80,3... | collective-permute-start | bytes 1179656 | tf_op jit(solution)/shard_map/ppermute | solution.py:220
  15.8 13.7 %collective-permute-start.4 = (bf16[512,384]{1,0:T(8,128)(2,1)S(1)}, bf16[512,384]{1,0:T(8,128)(2,1)S(1)}, u32[]{:S(2)}, u32[]{:S(2)}) collective-permute-start(bf16[512,384]{1,0:T(8,128)(2,1)S(1)} %collective-permute-done.1.refs_1_.refs_2_), channel_id=1, source_target_pairs={{2,0},{104,8},{18,16},{120,24},{6,4},{108,12},{22,20},{124,28},{34... | collective-permute-start | bytes 1179656 | tf_op jit(solution)/shard_map/ppermute | solution.py:220
  17.1 13.9 %collective-permute-start.6 = (bf16[512,384]{1,0:T(8,128)(2,1)S(1)}, bf16[512,384]{1,0:T(8,128)(2,1)S(1)}, u32[]{:S(2)}, u32[]{:S(2)}) collective-permute-start(bf16[512,384]{1,0:T(8,128)(2,1)S(1)} %collective-permute-done.1.refs_1_.refs_2_), channel_id=1, source_target_pairs={{96,0},{25,8},{112,16},{13,24},{100,4},{29,12},{116,20},{9,28},{0,... | collective-permute-start | bytes 1179656 | tf_op jit(solution)/shard_map/ppermute | solution.py:220
  22.7 13.3 %collective-permute-start.7 = (bf16[512,384]{1,0:T(8,128)(2,1)S(1)}, bf16[512,384]{1,0:T(8,128)(2,1)S(1)}, u32[]{:S(2)}, u32[]{:S(2)}) collective-permute-start(bf16[512,384]{1,0:T(8,128)(2,1)S(1)} %collective-permute-done.1.refs_1_.refs_2_), channel_id=1, source_target_pairs={{32,0},{31,8},{48,16},{11,24},{36,4},{27,12},{52,20},{15,28},{64,3... | collective-permute-start | bytes 1179656 | tf_op jit(solution)/shard_map/ppermute | solution.py:220
  22.7 8.0 %collective-permute-start.5 = (bf16[512,384]{1,0:T(8,128)(2,1)S(1)}, bf16[512,384]{1,0:T(8,128)(2,1)S(1)}, u32[]{:S(2)}, u32[]{:S(2)}) collective-permute-start(bf16[512,384]{1,0:T(8,128)(2,1)S(1)} %collective-permute-done.2.refs_2_.refs_3_), channel_id=1, source_target_pairs={{20,0},{24,8},{0,16},{12,24},{16,4},{28,12},{4,20},{8,28},{52,32},... | collective-permute-start | bytes 1179656 | tf_op jit(solution)/shard_map/ppermute | solution.py:220
  48.6 12.9 %collective-permute-start.12 = (bf16[512,128]{1,0:T(8,128)(2,1)S(1)}, bf16[512,128]{1,0:T(8,128)(2,1)S(1)}, u32[]{:S(2)}, u32[]{:S(2)}) collective-permute-start(bf16[512,128]{1,0:T(8,128)(2,1)S(1)} %get-tuple-element.24), channel_id=1, source_target_pairs={{0,5},{8,88},{16,21},{24,76},{4,1},{12,92},{20,17},{28,72},{32,37}... | collective-permute-start | bytes 393224 | tf_op jit(solution)/shard_map/ppermute | solution.py:237
  48.7 12.8 %collective-permute-start.11 = (bf16[512,128]{1,0:T(8,128)(2,1)S(1)}, bf16[512,128]{1,0:T(8,128)(2,1)S(1)}, u32[]{:S(2)}, u32[]{:S(2)}) collective-permute-start(bf16[512,128]{1,0:T(8,128)(2,1)S(1)} %get-tuple-element.23), channel_id=1, source_target_pairs={{0,97},{8,125},{16,113},{24,105},{4,101},{12,121},{20,117},{28,109... | collective-permute-start | bytes 393224 | tf_op jit(solution)/shard_map/ppermute | solution.py:237
  51.4 10.1 %collective-permute-start.10 = (bf16[512,128]{1,0:T(8,128)(2,1)S(1)}, bf16[512,128]{1,0:T(8,128)(2,1)S(1)}, u32[]{:S(2)}, u32[]{:S(2)}) collective-permute-start(bf16[512,128]{1,0:T(8,128)(2,1)S(1)} %get-tuple-element.22), channel_id=1, source_target_pairs={{0,48},{8,11},{16,36},{24,27},{4,52},{12,15},{20,32},{28,31},{32,8... | collective-permute-start | bytes 393224 | tf_op jit(solution)/shard_map/ppermute | solution.py:237
  55.5 6.0 %collective-permute-start.9 = (bf16[512,128]{1,0:T(8,128)(2,1)S(1)}, bf16[512,128]{1,0:T(8,128)(2,1)S(1)}, u32[]{:S(2)}, u32[]{:S(2)}) collective-permute-start(bf16[512,128]{1,0:T(8,128)(2,1)S(1)} %get-tuple-element.21), channel_id=1, source_target_pairs={{0,21},{8,72},{16,1},{24,88},{4,17},{12,76},{20,5},{28,92},{32,53}... | collective-permute-start | bytes 393224 | tf_op jit(solution)/shard_map/ppermute | solution.py:237
  58.3 5.9 %collective-permute-start.8 = (bf16[512,128]{1,0:T(8,128)(2,1)S(1)}, bf16[512,128]{1,0:T(8,128)(2,1)S(1)}, u32[]{:S(2)}, u32[]{:S(2)}) collective-permute-start(bf16[512,128]{1,0:T(8,128)(2,1)S(1)} %get-tuple-element.20), channel_id=1, source_target_pairs={{0,99},{8,29},{16,115},{24,9},{4,103},{12,25},{20,119},{28,13},{32... | collective-permute-start | bytes 393224 | tf_op jit(solution)/shard_map/ppermute | solution.py:237
  64.4 1.4 %collective-permute-start.13 = (f32[256,128]{1,0:T(8,128)S(1)}, f32[256,128]{1,0:T(8,128)S(1)}, u32[]{:S(2)}, u32[]{:S(2)}) collective-permute-start(f32[256,128]{1,0:T(8,128)S(1)} %slice.9), channel_id=1, source_target_pairs={{0,8},{8,0},{16,24},{24,16},{4,12},{12,4},{20,28},{28,20},{32,40},... | collective-permute-start | bytes 393224 | tf_op jit(solution)/shard_map/ppermute | solution.py:238

commit v6 on v3

--- a/solution.py
+++ b/solution.py
@@ -35,7 +35,7 @@
 ROWS = 512
 HALF = 256
 FEAT = 128
-UNROLL = 4
+UNROLL = 3
 ROW_TOTAL = FEAT + 3
 
 NEG_RATE = -math.sqrt(5.0) / math.log(2.0)
@@ -129,8 +129,10 @@
     left_x, right_x, left_v, right_v, turned, total, total_turned = refs
     for i in range(len(stage.ids)):
         prepare(i, chunks[i], stage, left_x, right_x, left_v, right_v, turned)
-    total[...] = jnp.zeros_like(total)
-    total_turned[...] = jnp.zeros_like(total_turned)
+    for i in range(len(stage.sums)):
+        total[i] = jnp.zeros(total.shape[1:], total.dtype)
+        if stage.count[0]:
+            total_turned[i] = jnp.zeros(total_turned.shape[1:], total_turned.dtype)
 
     def meet(a, b, rows, both):
         dist_sq = lax.dot_general(

time: 66.1 us -> 66.7 us (level)
  no operation moved by 1% of the time
where the time goes in v6:
time: 66.7 us; the launch traced here: 66.5 us
  starting transfers between devices  24.4 us (37%)
  Pallas kernels  22.9 us (34%)
  waiting for transfers between devices  16.3 us (24%)
  local copies, waits for them, and re-layouts  1.78 us (3%)
  other arithmetic  0.83 us (1%)
    pallas_call x3, Pallas kernels, sums_over_pairs(): pl.pallas_call(functools.partial(pair_kernel, stage, tuple(before)), out_...  22.9 us
    ppermute x7, starting transfers between devices, local(): chunks[i] = lax.ppermute(chunks[SOURCE[i]], AXES, shift(moves))  15.3 us
    ppermute x7, waiting for transfers between devices, local(): chunks[i] = lax.ppermute(chunks[SOURCE[i]], AXES, shift(moves))  11.1 us
    ppermute x5, starting transfers between devices, local(): lax.ppermute(sums[i], AXES, shift(moves, back=True)).astype(jnp.float32)  7.59 us
    ppermute x5, waiting for transfers between devices, local(): lax.ppermute(sums[i], AXES, shift(moves, back=True)).astype(jnp.float32)  2.78 us
    unnamed x18, local copies, waits for them, and re-layouts  1.75 us
    ppermute x1, starting transfers between devices, local(): lax.ppermute(mine, AXES, sibling())  1.5 us
    ppermute x1, waiting for transfers between devices, local(): return total[:HALF] + lax.ppermute(total[HALF:], AXES, sibling())  1.33 us
  transfers between devices with their start and end apart: 14, of which 7 were waited for; matrix products, arithmetic and copies ran while one was open for 0% of the time, Pallas kernels for 15%

profile of v6, /device:TPU:1, one launch (start us, length us, event | category | flops | bytes accessed | tf_op | source)
XLA Modules:
  0.0 66.5 jit_solution(4096294020148959152)
XLA Ops:
  0.0 0.0 copy-start
  0.0 0.9 %constant_dynamic-update-slice_fusion.2 = bf16[256,384]{1,0:T(8,128)(2,1)S(1)} fusion(bf16[256,128]{1,0:T(8,128)(2,1)} %param.9), kind=kLoop, calls=%fused_computation.5 | loop fusion | bytes 131072
  0.9 0.0 copy-done
  0.9 0.0 copy-start.1
  0.9 0.8 %copy-done.1 = bf16[256,128]{1,0:T(8,128)(2,1)S(1)} copy-done((bf16[256,128]{1,0:T(8,128)(2,1)S(1)}, bf16[256,128]{1,0:T(8,128)(2,1)}, u32[]{:S(2)}) %copy-start.1) | copy-done | bytes 65560
  1.8 1.5 %collective-permute-start = (bf16[256,384]{1,0:T(8,128)(2,1)S(1)}, bf16[256,384]{1,0:T(8,128)(2,1)S(1)}, u32[]{:S(2)}, u32[]{:S(2)}) collective-permute-start(bf16[256,384]{1,0:T(8,128)(2,1)S(1)} %constant_dynamic-update-slice_fusion), channel_id=1, source_target_pairs={{0,8},{8,0},{16,24},{24,16},{4,12},{12,4},{20,28},{28,20},{32,40},... | collective-permute-start | bytes 589832 | tf_op jit(solution)/shard_map/ppermute | solution.py:216
  3.3 0.0 copy-start.6
  3.3 0.0 copy-start.7
  3.3 1.1 %collective-permute-done = bf16[256,384]{1,0:T(8,128)(2,1)S(1)} collective-permute-done((bf16[256,384]{1,0:T(8,128)(2,1)S(1)}, bf16[256,384]{1,0:T(8,128)(2,1)S(1)}, u32[]{:S(2)}, u32[]{:S(2)}) %collective-permute-start) | collective-permute-done | bytes 196640 | tf_op jit(solution)/shard_map/ppermute | solution.py:216
  4.4 0.0 copy-start.4
  4.4 0.0 copy-start.5
  4.4 4.8 %collective-permute-start.1 = (bf16[512,384]{1,0:T(8,128)(2,1)S(1)}, bf16[512,384]{1,0:T(8,128)(2,1)S(1)}, u32[]{:S(2)}, u32[]{:S(2)}) collective-permute-start(bf16[512,384]{1,0:T(8,128)(2,1)S(1)} %pad_maximum_fusion.refs_0_), channel_id=1, source_target_pairs={{116,0},{27,8},{96,16},{15,24},{112,4},{31,12},{100,20},{11,28},{2... | collective-permute-start | bytes 1179656 | tf_op jit(solution)/shard_map/ppermute | solution.py:222
  9.2 2.9 %collective-permute-start.2 = (bf16[512,384]{1,0:T(8,128)(2,1)S(1)}, bf16[512,384]{1,0:T(8,128)(2,1)S(1)}, u32[]{:S(2)}, u32[]{:S(2)}) collective-permute-start(bf16[512,384]{1,0:T(8,128)(2,1)S(1)} %pad_maximum_fusion.refs_0_), channel_id=1, source_target_pairs={{19,0},{72,8},{7,16},{88,24},{23,4},{76,12},{3,20},{92,28},{51,32}... | collective-permute-start | bytes 1179656 | tf_op jit(solution)/shard_map/ppermute | solution.py:222
  12.2 0.0 copy-done.6
  12.2 0.0 copy-done.7
  12.2 0.0 copy-start.2
  12.2 0.0 copy-start.3
  12.2 0.1 collective-permute-start.3
  12.3 0.0 copy-done.4
  12.3 0.0 copy-done.5
  12.3 4.8 %collective-permute-done.1.refs_1_.refs_2_ = bf16[512,384]{1,0:T(8,128)(2,1)S(1)} collective-permute-done((bf16[512,384]{1,0:T(8,128)(2,1)S(1)}, bf16[512,384]{1,0:T(8,128)(2,1)S(1)}, u32[]{:S(2)}, u32[]{:S(2)}) %collective-permute-start.1) | collective-permute-done | bytes 393248 | tf_op jit(solution)/shard_map/ppermute | solution.py:222
  17.1 1.3 %collective-permute-start.4 = (bf16[512,384]{1,0:T(8,128)(2,1)S(1)}, bf16[512,384]{1,0:T(8,128)(2,1)S(1)}, u32[]{:S(2)}, u32[]{:S(2)}) collective-permute-start(bf16[512,384]{1,0:T(8,128)(2,1)S(1)} %collective-permute-done.1.refs_1_.refs_2_), channel_id=1, source_target_pairs={{4,0},{104,8},{20,16},{120,24},{0,4},{108,12},{16,20},{124,28},{36... | collective-permute-start | bytes 1179656 | tf_op jit(solution)/shard_map/ppermute | solution.py:222
  18.4 5.6 %collective-permute-start.6 = (bf16[512,384]{1,0:T(8,128)(2,1)S(1)}, bf16[512,384]{1,0:T(8,128)(2,1)S(1)}, u32[]{:S(2)}, u32[]{:S(2)}) collective-permute-start(bf16[512,384]{1,0:T(8,128)(2,1)S(1)} %collective-permute-done.1.refs_1_.refs_2_), channel_id=1, source_target_pairs={{96,0},{25,8},{112,16},{13,24},{100,4},{29,12},{116,20},{9,28},{0,... | collective-permute-start | bytes 1179656 | tf_op jit(solution)/shard_map/ppermute | solution.py:222
  24.0 0.0 collective-permute-start.7
  24.0 0.0 collective-permute-done.2.refs_2_.refs_3_
  24.0 0.6 collective-permute-start.5
  24.6 0.0 copy-done.2
  24.6 0.0 copy-done.3
  24.6 0.0 collective-permute-done.3.refs_3_.refs_4_
  24.6 6.6 %shard_map.91 = (f32[512,128]{1,0:T(8,128)S(1)}, f32[512,128]{1,0:T(8,128)S(1)}, f32[512,128]{1,0:T(8,128)S(1)}, f32[512,128]{1,0:T(8,128)S(1)}) custom-call(s32[12]{0:T(128)S(1)} %broadcast_select_fusion.2.table, bf16[512,384]{1,0:T(8,128)(2,1)S(1)} %pad_maximum_fusion.refs_0_, bf16[512,384]{1,0:T(8,128)(2,1)S(1)} %collective-permute-done.1.refs_1_.refs_2_, ...), custom_call_target="tpu_custom_call" | custom-call | flops 3221225472 | bytes 1572864 | tf_op jit(solution)/shard_map/pallas_call | solution.py:195
  31.2 0.0 collective-permute-done.4.refs_1_
  31.2 4.7 %collective-permute-done.5.refs_5_.refs_2_ = bf16[512,384]{1,0:T(8,128)(2,1)S(1)} collective-permute-done((bf16[512,384]{1,0:T(8,128)(2,1)S(1)}, bf16[512,384]{1,0:T(8,128)(2,1)S(1)}, u32[]{:S(2)}, u32[]{:S(2)}) %collective-permute-start.5) | collective-permute-done | bytes 393248 | tf_op jit(solution)/shard_map/ppermute | solution.py:222
  35.9 0.0 collective-permute-done.6.refs_6_.refs_3_
  35.9 1.7 %collective-permute-done.7.refs_7_.refs_4_ = bf16[512,384]{1,0:T(8,128)(2,1)S(1)} collective-permute-done((bf16[512,384]{1,0:T(8,128)(2,1)S(1)}, bf16[512,384]{1,0:T(8,128)(2,1)S(1)}, u32[]{:S(2)}, u32[]{:S(2)}) %collective-permute-start.7) | collective-permute-done | bytes 393248 | tf_op jit(solution)/shard_map/ppermute | solution.py:222
  37.5 13.2 %shard_map.92 = (f32[512,128]{1,0:T(8,128)S(1)}, bf16[512,128]{1,0:T(8,128)(2,1)S(1)}, bf16[512,128]{1,0:T(8,128)(2,1)S(1)}, bf16[512,128]{1,0:T(8,128)(2,1)S(1)...) custom-call(s32[28]{0:T(128)S(1)} %broadcast_select_fusion.1.table, ...), custom_call_target="tpu_custom_call" | custom-call | flops 7516192768 | bytes 3145728 | tf_op jit(solution)/shard_map/pallas_call | solution.py:195
  50.7 1.6 %collective-permute-start.12 = (bf16[512,128]{1,0:T(8,128)(2,1)S(1)}, bf16[512,128]{1,0:T(8,128)(2,1)S(1)}, u32[]{:S(2)}, u32[]{:S(2)}) collective-permute-start(bf16[512,128]{1,0:T(8,128)(2,1)S(1)} %get-tuple-element.24), channel_id=1, source_target_pairs={{0,18},{8,73},{16,6},{24,89},{4,22},{12,77},{20,2},{28,93},{32,50}... | collective-permute-start | bytes 393224 | tf_op jit(solution)/shard_map/ppermute | solution.py:239
  52.3 0.0 collective-permute-start.11
  52.3 5.2 %collective-permute-start.10 = (bf16[512,128]{1,0:T(8,128)(2,1)S(1)}, bf16[512,128]{1,0:T(8,128)(2,1)S(1)}, u32[]{:S(2)}, u32[]{:S(2)}) collective-permute-start(bf16[512,128]{1,0:T(8,128)(2,1)S(1)} %get-tuple-element.22), channel_id=1, source_target_pairs={{0,33},{8,28},{16,49},{24,8},{4,37},{12,24},{20,53},{28,12},{32,65... | collective-permute-start | bytes 393224 | tf_op jit(solution)/shard_map/ppermute | solution.py:239
  57.5 0.8 %collective-permute-start.9 = (bf16[512,128]{1,0:T(8,128)(2,1)S(1)}, bf16[512,128]{1,0:T(8,128)(2,1)S(1)}, u32[]{:S(2)}, u32[]{:S(2)}) collective-permute-start(bf16[512,128]{1,0:T(8,128)(2,1)S(1)} %get-tuple-element.21), channel_id=1, source_target_pairs={{0,19},{8,72},{16,7},{24,88},{4,23},{12,76},{20,3},{28,92},{32,51}... | collective-permute-start | bytes 393224 | tf_op jit(solution)/shard_map/ppermute | solution.py:239
  58.3 0.0 collective-permute-start.8
  58.3 3.1 %shard_map.93 = f32[512,128]{1,0:T(8,128)S(1)} custom-call(s32[6]{0:T(128)S(1)} %broadcast_select_fusion.table, bf16[512,384]{1,0:T(8,128)(2,1)S(1)} %pad_maximum_fusion.refs_0_, bf16[512,384]{1,0:T(8,128)(2,1)S(1)} %collective-permute-done.4.refs_1_, bf16[512,384]{1,0:T(8,128)(2,1)S(1)} %collective-permute-done.5.refs_5_.refs_2_, ...), custom_call_target="tpu_custom_call" | custom-call | flops 1610612736 | bytes 1966080 | tf_op jit(solution)/shard_map/pallas_call | solution.py:195
  61.4 0.0 collective-permute-done.12
  61.4 0.0 collective-permute-done.11
  61.5 0.0 collective-permute-done.10
  61.5 1.4 %collective-permute-done.9 = bf16[512,128]{1,0:T(8,128)(2,1)S(1)} collective-permute-done((bf16[512,128]{1,0:T(8,128)(2,1)S(1)}, bf16[512,128]{1,0:T(8,128)(2,1)S(1)}, u32[]{:S(2)}, u32[]{:S(2)}) %collective-permute-start.9) | collective-permute-done | bytes 131104 | tf_op jit(solution)/shard_map/ppermute | solution.py:239
  62.8 1.4 %collective-permute-done.8 = bf16[512,128]{1,0:T(8,128)(2,1)S(1)} collective-permute-done((bf16[512,128]{1,0:T(8,128)(2,1)S(1)}, bf16[512,128]{1,0:T(8,128)(2,1)S(1)}, u32[]{:S(2)}, u32[]{:S(2)}) %collective-permute-start.8) | collective-permute-done | bytes 131104 | tf_op jit(solution)/shard_map/ppermute | solution.py:239
  64.2 0.1 convert_add_fusion
  64.4 0.1 collective-permute-start.13
  64.5 1.3 %collective-permute-done.13 = f32[256,128]{1,0:T(8,128)S(1)} collective-permute-done((f32[256,128]{1,0:T(8,128)S(1)}, f32[256,128]{1,0:T(8,128)S(1)}, u32[]{:S(2)}, u32[]{:S(2)}) %collective-permute-start.13) | collective-permute-done | bytes 131104 | tf_op jit(solution)/shard_map/ppermute | solution.py:240
  65.8 0.7 %slice_add_fusion = f32[256,128]{1,0:T(8,128)} fusion(f32[256,128]{1,0:T(8,128)S(1)} %collective-permute-done.13, f32[512,128]{1,0:T(8,128)S(1)} %convert_add_fusion), kind=kLoop, calls=%fused_computation.2 | loop fusion | flops 32768 | bytes 393216 | tf_op jit(solution)/shard_map/add | solution.py:240
  (7 shorter events, 0.1 us)
Async XLA Ops:
  0.0 0.9 %copy-start = (bf16[256,128]{1,0:T(8,128)(2,1)S(1)}, bf16[256,128]{1,0:T(8,128)(2,1)}, u32[]{:S(2)}) copy-start(bf16[256,128]{1,0:T(8,128)(2,1)} %param.10) | copy-start | bytes 196612
  0.9 0.8 %copy-start.1 = (bf16[256,128]{1,0:T(8,128)(2,1)S(1)}, bf16[256,128]{1,0:T(8,128)(2,1)}, u32[]{:S(2)}) copy-start(bf16[256,128]{1,0:T(8,128)(2,1)} %param.11) | copy-start | bytes 196612
  1.8 2.6 %collective-permute-start = (bf16[256,384]{1,0:T(8,128)(2,1)S(1)}, bf16[256,384]{1,0:T(8,128)(2,1)S(1)}, u32[]{:S(2)}, u32[]{:S(2)}) collective-permute-start(bf16[256,384]{1,0:T(8,128)(2,1)S(1)} %constant_dynamic-update-slice_fusion), channel_id=1, source_target_pairs={{0,8},{8,0},{16,24},{24,16},{4,12},{12,4},{20,28},{28,20},{32,40},... | collective-permute-start | bytes 589832 | tf_op jit(solution)/shard_map/ppermute | solution.py:216
  3.3 8.9 %copy-start.6 = (s32[28]{0:T(128)S(1)}, s32[28]{0:T(128)}, u32[]{:S(2)}) copy-start(s32[28]{0:T(128)} %constant.34.clone) | copy-start | bytes 340
  3.3 8.9 %copy-start.7 = (s32[28]{0:T(128)S(1)}, s32[28]{0:T(128)}, u32[]{:S(2)}) copy-start(s32[28]{0:T(128)} %constant.35.clone) | copy-start | bytes 340
  4.4 7.9 %copy-start.4 = (s32[12]{0:T(128)S(1)}, s32[12]{0:T(128)}, u32[]{:S(2)}) copy-start(s32[12]{0:T(128)} %constant.32.clone) | copy-start | bytes 148
  4.4 7.9 %copy-start.5 = (s32[12]{0:T(128)S(1)}, s32[12]{0:T(128)}, u32[]{:S(2)}) copy-start(s32[12]{0:T(128)} %constant.33.clone) | copy-start | bytes 148
  4.4 12.7 %collective-permute-start.1 = (bf16[512,384]{1,0:T(8,128)(2,1)S(1)}, bf16[512,384]{1,0:T(8,128)(2,1)S(1)}, u32[]{:S(2)}, u32[]{:S(2)}) collective-permute-start(bf16[512,384]{1,0:T(8,128)(2,1)S(1)} %pad_maximum_fusion.refs_0_), channel_id=1, source_target_pairs={{116,0},{27,8},{96,16},{15,24},{112,4},{31,12},{100,20},{11,28},{2... | collective-permute-start | bytes 1179656 | tf_op jit(solution)/shard_map/ppermute | solution.py:222
  9.2 14.8 %collective-permute-start.2 = (bf16[512,384]{1,0:T(8,128)(2,1)S(1)}, bf16[512,384]{1,0:T(8,128)(2,1)S(1)}, u32[]{:S(2)}, u32[]{:S(2)}) collective-permute-start(bf16[512,384]{1,0:T(8,128)(2,1)S(1)} %pad_maximum_fusion.refs_0_), channel_id=1, source_target_pairs={{19,0},{72,8},{7,16},{88,24},{23,4},{76,12},{3,20},{92,28},{51,32}... | collective-permute-start | bytes 1179656 | tf_op jit(solution)/shard_map/ppermute | solution.py:222
  12.2 12.4 %copy-start.2 = (s32[6]{0:T(128)S(1)}, s32[6]{0:T(128)}, u32[]{:S(2)}) copy-start(s32[6]{0:T(128)} %constant.36.clone) | copy-start | bytes 76
  12.2 12.4 %copy-start.3 = (s32[6]{0:T(128)S(1)}, s32[6]{0:T(128)}, u32[]{:S(2)}) copy-start(s32[6]{0:T(128)} %constant.37.clone) | copy-start | bytes 76
  12.2 12.4 %collective-permute-start.3 = (bf16[512,384]{1,0:T(8,128)(2,1)S(1)}, bf16[512,384]{1,0:T(8,128)(2,1)S(1)}, u32[]{:S(2)}, u32[]{:S(2)}) collective-permute-start(bf16[512,384]{1,0:T(8,128)(2,1)S(1)} %pad_maximum_fusion.refs_0_), channel_id=1, source_target_pairs={{33,0},{28,8},{49,16},{8,24},{37,4},{24,12},{53,20},{12,28},{65,32... | collective-permute-start | bytes 1179656 | tf_op jit(solution)/shard_map/ppermute | solution.py:222
  17.1 14.1 %collective-permute-start.4 = (bf16[512,384]{1,0:T(8,128)(2,1)S(1)}, bf16[512,384]{1,0:T(8,128)(2,1)S(1)}, u32[]{:S(2)}, u32[]{:S(2)}) collective-permute-start(bf16[512,384]{1,0:T(8,128)(2,1)S(1)} %collective-permute-done.1.refs_1_.refs_2_), channel_id=1, source_target_pairs={{4,0},{104,8},{20,16},{120,24},{0,4},{108,12},{16,20},{124,28},{36... | collective-permute-start | bytes 1179656 | tf_op jit(solution)/shard_map/ppermute | solution.py:222
  18.4 17.5 %collective-permute-start.6 = (bf16[512,384]{1,0:T(8,128)(2,1)S(1)}, bf16[512,384]{1,0:T(8,128)(2,1)S(1)}, u32[]{:S(2)}, u32[]{:S(2)}) collective-permute-start(bf16[512,384]{1,0:T(8,128)(2,1)S(1)} %collective-permute-done.1.refs_1_.refs_2_), channel_id=1, source_target_pairs={{96,0},{25,8},{112,16},{13,24},{100,4},{29,12},{116,20},{9,28},{0,... | collective-permute-start | bytes 1179656 | tf_op jit(solution)/shard_map/ppermute | solution.py:222
  24.0 13.5 %collective-permute-start.7 = (bf16[512,384]{1,0:T(8,128)(2,1)S(1)}, bf16[512,384]{1,0:T(8,128)(2,1)S(1)}, u32[]{:S(2)}, u32[]{:S(2)}) collective-permute-start(bf16[512,384]{1,0:T(8,128)(2,1)S(1)} %collective-permute-done.1.refs_1_.refs_2_), channel_id=1, source_target_pairs={{32,0},{31,8},{48,16},{11,24},{36,4},{27,12},{52,20},{15,28},{64,3... | collective-permute-start | bytes 1179656 | tf_op jit(solution)/shard_map/ppermute | solution.py:222
  24.0 11.9 %collective-permute-start.5 = (bf16[512,384]{1,0:T(8,128)(2,1)S(1)}, bf16[512,384]{1,0:T(8,128)(2,1)S(1)}, u32[]{:S(2)}, u32[]{:S(2)}) collective-permute-start(bf16[512,384]{1,0:T(8,128)(2,1)S(1)} %collective-permute-done.2.refs_2_.refs_3_), channel_id=1, source_target_pairs={{3,0},{9,8},{19,16},{25,24},{7,4},{13,12},{23,20},{29,28},{35,32},... | collective-permute-start | bytes 1179656 | tf_op jit(solution)/shard_map/ppermute | solution.py:222
  50.7 10.7 %collective-permute-start.12 = (bf16[512,128]{1,0:T(8,128)(2,1)S(1)}, bf16[512,128]{1,0:T(8,128)(2,1)S(1)}, u32[]{:S(2)}, u32[]{:S(2)}) collective-permute-start(bf16[512,128]{1,0:T(8,128)(2,1)S(1)} %get-tuple-element.24), channel_id=1, source_target_pairs={{0,18},{8,73},{16,6},{24,89},{4,22},{12,77},{20,2},{28,93},{32,50}... | collective-permute-start | bytes 393224 | tf_op jit(solution)/shard_map/ppermute | solution.py:239
  52.3 9.1 %collective-permute-start.11 = (bf16[512,128]{1,0:T(8,128)(2,1)S(1)}, bf16[512,128]{1,0:T(8,128)(2,1)S(1)}, u32[]{:S(2)}, u32[]{:S(2)}) collective-permute-start(bf16[512,128]{1,0:T(8,128)(2,1)S(1)} %get-tuple-element.23), channel_id=1, source_target_pairs={{0,112},{8,123},{16,100},{24,111},{4,116},{12,127},{20,96},{28,107... | collective-permute-start | bytes 393224 | tf_op jit(solution)/shard_map/ppermute | solution.py:239
  52.3 9.1 %collective-permute-start.10 = (bf16[512,128]{1,0:T(8,128)(2,1)S(1)}, bf16[512,128]{1,0:T(8,128)(2,1)S(1)}, u32[]{:S(2)}, u32[]{:S(2)}) collective-permute-start(bf16[512,128]{1,0:T(8,128)(2,1)S(1)} %get-tuple-element.22), channel_id=1, source_target_pairs={{0,33},{8,28},{16,49},{24,8},{4,37},{12,24},{20,53},{28,12},{32,65... | collective-permute-start | bytes 393224 | tf_op jit(solution)/shard_map/ppermute | solution.py:239
  57.5 5.3 %collective-permute-start.9 = (bf16[512,128]{1,0:T(8,128)(2,1)S(1)}, bf16[512,128]{1,0:T(8,128)(2,1)S(1)}, u32[]{:S(2)}, u32[]{:S(2)}) collective-permute-start(bf16[512,128]{1,0:T(8,128)(2,1)S(1)} %get-tuple-element.21), channel_id=1, source_target_pairs={{0,19},{8,72},{16,7},{24,88},{4,23},{12,76},{20,3},{28,92},{32,51}... | collective-permute-start | bytes 393224 | tf_op jit(solution)/shard_map/ppermute | solution.py:239
  58.3 5.9 %collective-permute-start.8 = (bf16[512,128]{1,0:T(8,128)(2,1)S(1)}, bf16[512,128]{1,0:T(8,128)(2,1)S(1)}, u32[]{:S(2)}, u32[]{:S(2)}) collective-permute-start(bf16[512,128]{1,0:T(8,128)(2,1)S(1)} %get-tuple-element.20), channel_id=1, source_target_pairs={{0,116},{8,27},{16,96},{24,15},{4,112},{12,31},{20,100},{28,11},{3... | collective-permute-start | bytes 393224 | tf_op jit(solution)/shard_map/ppermute | solution.py:239
  64.4 1.4 %collective-permute-start.13 = (f32[256,128]{1,0:T(8,128)S(1)}, f32[256,128]{1,0:T(8,128)S(1)}, u32[]{:S(2)}, u32[]{:S(2)}) collective-permute-start(f32[256,128]{1,0:T(8,128)S(1)} %slice.9), channel_id=1, source_target_pairs={{0,8},{8,0},{16,24},{24,16},{4,12},{12,4},{20,28},{28,20},{32,40},... | collective-permute-start | bytes 393224 | tf_op jit(solution)/shard_map/ppermute | solution.py:240
